TPU v7x, 32 devices: a whole 2x2x4 slice. The times are simulated.
32 devices in a mesh: groups: 2 (over x), cells: 16 (over z, y, core).
Axes of the slice: x: 2, y: 2, z: 4, core: 2. Of those that a mesh axis runs over, the one named last changes fastest.
Arguments:
- footprints: bfloat16 [256, 128, 128], P(('groups', 'cells')), parts along dimension 0, may hold values from -0.1875 to 0.1875
- tile_rows: int32 [256], P(('groups', 'cells')), parts along dimension 0, may hold values from 0 to 7
- tile_cols: int32 [256], P(('groups', 'cells')), parts along dimension 0, may hold values from 0 to 15
- tile_counts: int32 [32], P(('groups', 'cells')), parts along dimension 0, may hold values from 1 to 8, as said below
- coords: float32 [2, 8192], P(None, ('groups', 'cells')), parts along dimension 1, may hold values from 0 to 3
- obs_error: float32 [2048], P(('groups', 'cells')), parts along dimension 0, may hold values from 0.5 to 2
Outputs:
- covariance: float32 [2048, 1024], P(('groups', 'cells')), parts along dimension 0
There are 2 independent parts, one for each index of `groups`. A program takes and returns all parts, laid end to end along the dimension named above; each array names one. Nothing has to cross between parts.
Inputs may be any that keep to these rules, and one draw needn't show every extreme that they name: The first tile_counts[c] slots of device c are live, the rest are ignored; in every draw some device has all 8 slots live.
All inputs are finite; a program needn't handle non-finite values.
Results may differ from a plain program's by a relative error of at most 0.0038.
Values may be sent and summed in bfloat16 or wider, within the bound.
A program may use at most 64 MiB of HBM per device.

v0:
```python
import jax
import jax.numpy as jnp
from jax import lax
from jax.sharding import PartitionSpec as P

WEEKS = 8
OBS = 1024


SPACE_RANGE = 1.0
TIME_RANGE = 3.0


def from_behind(value, axis, steps):
    count = lax.axis_size(axis)
    pairs = [(source, (source + steps) % count) for source in range(count)]
    return lax.ppermute(value, axis, pairs)


def space_block(home_pos, visitor_pos):
    east_gap = home_pos[0][:, None] - visitor_pos[0][None, :]
    north_gap = home_pos[1][:, None] - visitor_pos[1][None, :]
    return jnp.exp(-jnp.sqrt(east_gap * east_gap + north_gap * north_gap) / SPACE_RANGE).astype(
        jnp.bfloat16
    )


def absorb(accumulator, tile_stack, row_index, col_index, live_count, covar):
    slot_count, tile_edge = (tile_stack.shape[0], tile_stack.shape[1])
    cell_count = accumulator.shape[2]
    per_week = cell_count // tile_edge
    week_index = col_index // per_week
    cell_block = col_index % per_week
    strips = jnp.take(covar.reshape(cell_count, per_week, tile_edge), cell_block, axis=1)
    products = jnp.einsum("isj,smj->sim", strips, tile_stack, preferred_element_type=jnp.float32)
    live = jnp.arange(slot_count, dtype=jnp.int32) < live_count
    products = jnp.where(live[:, None, None], products, jnp.zeros_like(products))
    return accumulator.at[week_index, row_index].add(products)


def visit(accumulator, home_pos, tile_stack, visitor_pos, row_index, col_index, live_count):
    return absorb(
        accumulator,
        tile_stack,
        row_index,
        col_index,
        live_count,
        space_block(home_pos, visitor_pos),
    )


def own_rows(running, weighted, tile_stack, row_index, col_index, live_count):
    slot_count, tile_edge = (tile_stack.shape[0], tile_stack.shape[1])
    weeks, row_tiles, cell_count, _ = weighted.shape
    per_week = cell_count // tile_edge
    week_index = col_index // per_week
    cell_block = col_index % per_week
    shaped = weighted.reshape(weeks, row_tiles, per_week, tile_edge, tile_edge)
    strips = shaped[week_index, :, cell_block]
    partial_value = jnp.einsum(
        "smj,srjn->smrn", tile_stack, strips, preferred_element_type=jnp.float32
    )
    partial_value = partial_value.reshape(slot_count, tile_edge, row_tiles * tile_edge)
    live = jnp.arange(slot_count, dtype=jnp.int32) < live_count
    partial_value = jnp.where(live[:, None, None], partial_value, jnp.zeros_like(partial_value))
    blocked = running.reshape(running.shape[0] // tile_edge, tile_edge, running.shape[1])
    blocked = blocked.at[row_index].add(partial_value)
    return blocked.reshape(running.shape)


def local(footprints, tile_rows, tile_cols, tile_counts, coords, obs_error):
    cell_count = coords.shape[1]
    tile_edge = footprints.shape[1]
    accumulator = jnp.zeros((WEEKS, OBS // tile_edge, cell_count, tile_edge), jnp.float32)
    accumulator = visit(
        accumulator, coords, footprints, coords, tile_rows, tile_cols, tile_counts[0]
    )

    def hop(hop_number, cycle_state):
        accumulator, tile_stack, visitor_pos, row_index, col_index, counts = cycle_state
        tile_stack = from_behind(tile_stack, "cells", 1)
        visitor_pos = from_behind(visitor_pos, "cells", 1)
        row_index, col_index, counts = from_behind((row_index, col_index, counts), "cells", 1)
        accumulator = visit(
            accumulator, coords, tile_stack, visitor_pos, row_index, col_index, counts[0]
        )
        return (accumulator, tile_stack, visitor_pos, row_index, col_index, counts)

    cycle_state = (accumulator, footprints, coords, tile_rows, tile_cols, tile_counts)
    accumulator = lax.fori_loop(0, lax.axis_size("cells") - 1, hop, cycle_state)[0]
    week_axis = jnp.arange(WEEKS).astype(jnp.float32)
    time_cov = jnp.exp(-jnp.abs(week_axis[:, None] - week_axis[None, :]) / TIME_RANGE)
    weighted = jnp.einsum(
        "wv,vrim->wrim", time_cov, accumulator, precision=lax.Precision.HIGHEST
    ).astype(jnp.bfloat16)
    running = own_rows(
        jnp.zeros((OBS, OBS), jnp.float32),
        weighted,
        footprints,
        tile_rows,
        tile_cols,
        tile_counts[0],
    )
    summed = lax.psum_scatter(running, "cells", scatter_dimension=0, tiled=True)
    row_offset = lax.axis_index("cells") * summed.shape[0]
    diagonal_mask = lax.broadcasted_iota(
        jnp.int32, summed.shape, 1
    ) == row_offset + lax.broadcasted_iota(jnp.int32, summed.shape, 0)
    return summed + jnp.where(diagonal_mask, obs_error[:, None], 0.0)


def solution(mesh):
    placed = (
        P(("groups", "cells"), None, None),
        P(("groups", "cells")),
        P(("groups", "cells")),
        P(("groups", "cells")),
        P(None, ("groups", "cells")),
        P(("groups", "cells")),
    )
    return jax.shard_map(
        local, mesh=mesh, in_specs=placed, out_specs=P(("groups", "cells"), None), check_vma=False
    )
```

profile of v0, /device:TPU:0, one launch (start us, length us, event | category | flops | bytes accessed | tf_op | source)
XLA Modules:
  0.0 371.3 jit_solution(12317144320989024075)
XLA Ops:
  12.2 4.3 %broadcast_in_dim.80 = f32[8,8,256,128]{3,2,1,0:T(8,128)} broadcast(f32[]{:T(128)} %constant.105.clone.1), dimensions={} | broadcast | bytes 8388612 | tf_op jit(solution)/shard_map/broadcast_in_dim | solution.py:74
  16.5 3.4 scatter_fusion.1
  19.9 225.0 %while.22 = (s32[]{:T(128)}, f32[8,8,256,128]{3,2,1,0:T(8,128)}, bf16[8,128,128]{2,1,0:T(8,128)(2,1)S(1)}, f32[2,256]{1,0:T(2,128)S(1)}, s32[8]{0:T(128)S(1)}, /...) while((s32[]{:T(128)}, f32[8,8,256,128]{3,2,1,0:T(8,128)}, ...), condition=%wide.region_3.5_spmd, body=%wide.region_1.4_spmd.sunk | while | flops 68355456 | bytes 7762945 | solution.py:90
  20.3 2.6 collective-permute-start.1
  23.0 2.4 collective-permute-start.2
  25.4 2.5 collective-permute-start
  28.0 3.5 collective-permute-done.2
  33.5 3.4 scatter_fusion
  39.8 2.5 collective-permute-start
  42.4 3.9 %collective-permute-done.2 = s32[1]{0:T(128)} collective-permute-done((s32[1]{0:T(128)}, s32[1]{0:T(128)}, u32[]{:S(2)}, u32[]{:S(2)}) %collective-permute-start.2) | collective-permute-done | bytes 36 | tf_op jit(solution)/shard_map/while/body/eval_jaxpr/ppermute | solution.py:17
  48.3 3.3 scatter_fusion
  53.7 2.4 collective-permute-start
  56.1 5.0 %collective-permute-done.2 = s32[1]{0:T(128)} collective-permute-done((s32[1]{0:T(128)}, s32[1]{0:T(128)}, u32[]{:S(2)}, u32[]{:S(2)}) %collective-permute-start.2) | collective-permute-done | bytes 36 | tf_op jit(solution)/shard_map/while/body/eval_jaxpr/ppermute | solution.py:17
  63.1 3.4 scatter_fusion
  68.5 2.1 collective-permute-start
  70.7 5.2 %collective-permute-done.2 = s32[1]{0:T(128)} collective-permute-done((s32[1]{0:T(128)}, s32[1]{0:T(128)}, u32[]{:S(2)}, u32[]{:S(2)}) %collective-permute-start.2) | collective-permute-done | bytes 36 | tf_op jit(solution)/shard_map/while/body/eval_jaxpr/ppermute | solution.py:17
  77.9 3.4 scatter_fusion
  84.2 6.5 %collective-permute-done.2 = s32[1]{0:T(128)} collective-permute-done((s32[1]{0:T(128)}, s32[1]{0:T(128)}, u32[]{:S(2)}, u32[]{:S(2)}) %collective-permute-start.2) | collective-permute-done | bytes 36 | tf_op jit(solution)/shard_map/while/body/eval_jaxpr/ppermute | solution.py:17
  92.7 3.3 scatter_fusion
  98.6 6.8 %collective-permute-done.2 = s32[1]{0:T(128)} collective-permute-done((s32[1]{0:T(128)}, s32[1]{0:T(128)}, u32[]{:S(2)}, u32[]{:S(2)}) %collective-permute-start.2) | collective-permute-done | bytes 36 | tf_op jit(solution)/shard_map/while/body/eval_jaxpr/ppermute | solution.py:17
  107.5 3.4 scatter_fusion
  113.0 7.3 %collective-permute-done.2 = s32[1]{0:T(128)} collective-permute-done((s32[1]{0:T(128)}, s32[1]{0:T(128)}, u32[]{:S(2)}, u32[]{:S(2)}) %collective-permute-start.2) | collective-permute-done | bytes 36 | tf_op jit(solution)/shard_map/while/body/eval_jaxpr/ppermute | solution.py:17
  122.3 3.4 scatter_fusion
  127.8 7.3 %collective-permute-done.2 = s32[1]{0:T(128)} collective-permute-done((s32[1]{0:T(128)}, s32[1]{0:T(128)}, u32[]{:S(2)}, u32[]{:S(2)}) %collective-permute-start.2) | collective-permute-done | bytes 36 | tf_op jit(solution)/shard_map/while/body/eval_jaxpr/ppermute | solution.py:17
  137.2 3.3 scatter_fusion
  142.6 7.3 %collective-permute-done.2 = s32[1]{0:T(128)} collective-permute-done((s32[1]{0:T(128)}, s32[1]{0:T(128)}, u32[]{:S(2)}, u32[]{:S(2)}) %collective-permute-start.2) | collective-permute-done | bytes 36 | tf_op jit(solution)/shard_map/while/body/eval_jaxpr/ppermute | solution.py:17
  151.9 3.4 scatter_fusion
  157.4 7.3 %collective-permute-done.2 = s32[1]{0:T(128)} collective-permute-done((s32[1]{0:T(128)}, s32[1]{0:T(128)}, u32[]{:S(2)}, u32[]{:S(2)}) %collective-permute-start.2) | collective-permute-done | bytes 36 | tf_op jit(solution)/shard_map/while/body/eval_jaxpr/ppermute | solution.py:17
  166.8 3.4 scatter_fusion
  172.2 7.3 %collective-permute-done.2 = s32[1]{0:T(128)} collective-permute-done((s32[1]{0:T(128)}, s32[1]{0:T(128)}, u32[]{:S(2)}, u32[]{:S(2)}) %collective-permute-start.2) | collective-permute-done | bytes 36 | tf_op jit(solution)/shard_map/while/body/eval_jaxpr/ppermute | solution.py:17
  181.6 3.4 scatter_fusion
  187.1 7.3 %collective-permute-done.2 = s32[1]{0:T(128)} collective-permute-done((s32[1]{0:T(128)}, s32[1]{0:T(128)}, u32[]{:S(2)}, u32[]{:S(2)}) %collective-permute-start.2) | collective-permute-done | bytes 36 | tf_op jit(solution)/shard_map/while/body/eval_jaxpr/ppermute | solution.py:17
  196.5 3.4 scatter_fusion
  201.9 7.3 %collective-permute-done.2 = s32[1]{0:T(128)} collective-permute-done((s32[1]{0:T(128)}, s32[1]{0:T(128)}, u32[]{:S(2)}, u32[]{:S(2)}) %collective-permute-start.2) | collective-permute-done | bytes 36 | tf_op jit(solution)/shard_map/while/body/eval_jaxpr/ppermute | solution.py:17
  211.3 3.3 scatter_fusion
  216.7 7.3 %collective-permute-done.2 = s32[1]{0:T(128)} collective-permute-done((s32[1]{0:T(128)}, s32[1]{0:T(128)}, u32[]{:S(2)}, u32[]{:S(2)}) %collective-permute-start.2) | collective-permute-done | bytes 36 | tf_op jit(solution)/shard_map/while/body/eval_jaxpr/ppermute | solution.py:17
  226.0 3.4 scatter_fusion
  231.5 7.3 %collective-permute-done.2 = s32[1]{0:T(128)} collective-permute-done((s32[1]{0:T(128)}, s32[1]{0:T(128)}, u32[]{:S(2)}, u32[]{:S(2)}) %collective-permute-start.2) | collective-permute-done | bytes 36 | tf_op jit(solution)/shard_map/while/body/eval_jaxpr/ppermute | solution.py:17
  240.9 3.4 scatter_fusion
  244.9 15.3 %fusion.14 = bf16[8,8,256,128]{3,0,2,1:T(8,128)(2,1)S(1)} fusion(f32[8,8,256,128]{3,2,1,0:T(8,128)} %get-tuple-element.110, f32[8]{0:T(128)S(1)} %iota_convert_fusion), kind=kOutput, calls=%fused_computation.34 | convolution fusion | flops 203424000 | bytes 12582944 | tf_op jit(solution)/shard_map/wv,vrim->wrim/dot_general | solution.py:93
  260.2 3.0 copy.10
  263.3 3.2 gather_fusion.1
  266.5 2.8 fusion.20
  269.2 5.4 %copy.12 = f32[8,128,1024]{2,1,0:T(8,128)} copy(f32[8,128,1024]{1,2,0:T(8,128)} %bitcast.90) | data formatting | bytes 8388608 | tf_op jit(solution)/shard_map/reshape | solution.py:63
  274.6 5.1 %broadcast_select_fusion.1 = f32[8,128,1024]{2,1,0:T(8,128)} fusion(f32[8,128,1024]{2,1,0:T(8,128)} %copy.12, pred[8]{0:T(512)(128)(4,1)S(1)} %get-tuple-element.139), kind=kLoop, calls=%fused_computation.35 | loop fusion | flops 1048576 | bytes 8388616 | tf_op jit(solution)/shard_map/jit(_where)/select_n | solution.py:65
  279.7 2.5 broadcast.134
  282.1 9.2 %scatter_fusion.2 = f32[8,128,1024]{2,1,0:T(8,128)} fusion(f32[8,128,1024]{2,1,0:T(8,128)} %broadcast.134, s32[8]{0:T(128)S(1)} %compare_select_fusion.8, f32[8,128,1024]{2,1,0:T(8,128)} %broadcast_select_fusion.1), kind=kCustom, calls=%fused_computation.5 | custom fusion | flops 1048576 | bytes 12582944 | tf_op jit(solution)/shard_map/scatter-add | solution.py:67
  291.4 71.3 %reduce-scatter.2.cloned.1.call-done = f32[64,1024]{1,0:T(8,128)} async-done(((f32[1024,1024]{1,0:T(8,128)}), f32[64,1024]{1,0:T(8,128)}) %reduce-scatter.2.cloned.1.call-update) | async-done | bytes 262160 | tf_op jit(solution)/shard_map/reduce_scatter | solution.py:104
  (349 shorter events, 57.4 us)
Async XLA Ops:
  6.5 356.2 %reduce-scatter.2.cloned.1.call-start = ((), (), s32[]{:S(2)}) async-start(), calls=%async_computation.1 | async-start | bytes 4456448 | tf_op jit(solution)/shard_map/reduce_scatter | solution.py:104
  19.9 12.3 %collective-permute-start.4 = (f32[2,256]{1,0:T(2,128)S(1)}, f32[2,256]{1,0:T(2,128)S(1)}, u32[]{:S(2)}, u32[]{:S(2)}) collective-permute-start(f32[2,256]{1,0:T(2,128)S(1)} %get-tuple-element.213), channel_id=1, source_target_pairs={{0,1},{1,2},{2,3},{3,4},{4,5},{5,6},{6,7},{7,8},{8,9},{9,10},{10,1... | collective-permute-start | bytes 6152 | tf_op jit(solution)/shard_map/while/body/eval_jaxpr/ppermute | solution.py:17
  20.3 11.8 %collective-permute-start.1 = (s32[8]{0:T(128)S(1)}, s32[8]{0:T(128)S(1)}, u32[]{:S(2)}, u32[]{:S(2)}) collective-permute-start(s32[8]{0:T(128)S(1)} %get-tuple-element.215), channel_id=1, source_target_pairs={{0,1},{1,2},{2,3},{3,4},{4,5},{5,6},{6,7},{7,8},{8,9},{9,10},{10,1... | collective-permute-start | bytes 104 | tf_op jit(solution)/shard_map/while/body/eval_jaxpr/ppermute | solution.py:17
  22.9 10.2 %collective-permute-start.3 = (bf16[8,128,128]{2,1,0:T(8,128)(2,1)S(1)}, bf16[8,128,128]{2,1,0:T(8,128)(2,1)S(1)}, u32[]{:S(2)}, u32[]{:S(2)}) collective-permute-start(bf16[8,128,128]{2,1,0:T(8,128)(2,1)S(1)} %get-tuple-element.212), channel_id=1, source_target_pairs={{0,1},{1,2},{2,3},{3,4},{4,5},{5,6},{6,7},{7,8},{8,9},{9,10},{10,1... | collective-permute-start | bytes 786440 | tf_op jit(solution)/shard_map/while/body/eval_jaxpr/ppermute | solution.py:17
  37.6 9.5 %collective-permute-start.4 = (f32[2,256]{1,0:T(2,128)S(1)}, f32[2,256]{1,0:T(2,128)S(1)}, u32[]{:S(2)}, u32[]{:S(2)}) collective-permute-start(f32[2,256]{1,0:T(2,128)S(1)} %get-tuple-element.213), channel_id=1, source_target_pairs={{0,1},{1,2},{2,3},{3,4},{4,5},{5,6},{6,7},{7,8},{8,9},{9,10},{10,1... | collective-permute-start | bytes 6152 | tf_op jit(solution)/shard_map/while/body/eval_jaxpr/ppermute | solution.py:17
  37.6 9.3 %collective-permute-start.1 = (s32[8]{0:T(128)S(1)}, s32[8]{0:T(128)S(1)}, u32[]{:S(2)}, u32[]{:S(2)}) collective-permute-start(s32[8]{0:T(128)S(1)} %get-tuple-element.215), channel_id=1, source_target_pairs={{0,1},{1,2},{2,3},{3,4},{4,5},{5,6},{6,7},{7,8},{8,9},{9,10},{10,1... | collective-permute-start | bytes 104 | tf_op jit(solution)/shard_map/while/body/eval_jaxpr/ppermute | solution.py:17
  37.7 10.2 %collective-permute-start.3 = (bf16[8,128,128]{2,1,0:T(8,128)(2,1)S(1)}, bf16[8,128,128]{2,1,0:T(8,128)(2,1)S(1)}, u32[]{:S(2)}, u32[]{:S(2)}) collective-permute-start(bf16[8,128,128]{2,1,0:T(8,128)(2,1)S(1)} %get-tuple-element.212), channel_id=1, source_target_pairs={{0,1},{1,2},{2,3},{3,4},{4,5},{5,6},{6,7},{7,8},{8,9},{9,10},{10,1... | collective-permute-start | bytes 786440 | tf_op jit(solution)/shard_map/while/body/eval_jaxpr/ppermute | solution.py:17
  52.3 9.5 %collective-permute-start.4 = (f32[2,256]{1,0:T(2,128)S(1)}, f32[2,256]{1,0:T(2,128)S(1)}, u32[]{:S(2)}, u32[]{:S(2)}) collective-permute-start(f32[2,256]{1,0:T(2,128)S(1)} %get-tuple-element.213), channel_id=1, source_target_pairs={{0,1},{1,2},{2,3},{3,4},{4,5},{5,6},{6,7},{7,8},{8,9},{9,10},{10,1... | collective-permute-start | bytes 6152 | tf_op jit(solution)/shard_map/while/body/eval_jaxpr/ppermute | solution.py:17
  52.4 9.3 %collective-permute-start.1 = (s32[8]{0:T(128)S(1)}, s32[8]{0:T(128)S(1)}, u32[]{:S(2)}, u32[]{:S(2)}) collective-permute-start(s32[8]{0:T(128)S(1)} %get-tuple-element.215), channel_id=1, source_target_pairs={{0,1},{1,2},{2,3},{3,4},{4,5},{5,6},{6,7},{7,8},{8,9},{9,10},{10,1... | collective-permute-start | bytes 104 | tf_op jit(solution)/shard_map/while/body/eval_jaxpr/ppermute | solution.py:17
  52.5 10.2 %collective-permute-start.3 = (bf16[8,128,128]{2,1,0:T(8,128)(2,1)S(1)}, bf16[8,128,128]{2,1,0:T(8,128)(2,1)S(1)}, u32[]{:S(2)}, u32[]{:S(2)}) collective-permute-start(bf16[8,128,128]{2,1,0:T(8,128)(2,1)S(1)} %get-tuple-element.212), channel_id=1, source_target_pairs={{0,1},{1,2},{2,3},{3,4},{4,5},{5,6},{6,7},{7,8},{8,9},{9,10},{10,1... | collective-permute-start | bytes 786440 | tf_op jit(solution)/shard_map/while/body/eval_jaxpr/ppermute | solution.py:17
  67.2 9.5 %collective-permute-start.4 = (f32[2,256]{1,0:T(2,128)S(1)}, f32[2,256]{1,0:T(2,128)S(1)}, u32[]{:S(2)}, u32[]{:S(2)}) collective-permute-start(f32[2,256]{1,0:T(2,128)S(1)} %get-tuple-element.213), channel_id=1, source_target_pairs={{0,1},{1,2},{2,3},{3,4},{4,5},{5,6},{6,7},{7,8},{8,9},{9,10},{10,1... | collective-permute-start | bytes 6152 | tf_op jit(solution)/shard_map/while/body/eval_jaxpr/ppermute | solution.py:17
  67.2 9.3 %collective-permute-start.1 = (s32[8]{0:T(128)S(1)}, s32[8]{0:T(128)S(1)}, u32[]{:S(2)}, u32[]{:S(2)}) collective-permute-start(s32[8]{0:T(128)S(1)} %get-tuple-element.215), channel_id=1, source_target_pairs={{0,1},{1,2},{2,3},{3,4},{4,5},{5,6},{6,7},{7,8},{8,9},{9,10},{10,1... | collective-permute-start | bytes 104 | tf_op jit(solution)/shard_map/while/body/eval_jaxpr/ppermute | solution.py:17
  67.3 10.2 %collective-permute-start.3 = (bf16[8,128,128]{2,1,0:T(8,128)(2,1)S(1)}, bf16[8,128,128]{2,1,0:T(8,128)(2,1)S(1)}, u32[]{:S(2)}, u32[]{:S(2)}) collective-permute-start(bf16[8,128,128]{2,1,0:T(8,128)(2,1)S(1)} %get-tuple-element.212), channel_id=1, source_target_pairs={{0,1},{1,2},{2,3},{3,4},{4,5},{5,6},{6,7},{7,8},{8,9},{9,10},{10,1... | collective-permute-start | bytes 786440 | tf_op jit(solution)/shard_map/while/body/eval_jaxpr/ppermute | solution.py:17
  82.0 9.5 %collective-permute-start.4 = (f32[2,256]{1,0:T(2,128)S(1)}, f32[2,256]{1,0:T(2,128)S(1)}, u32[]{:S(2)}, u32[]{:S(2)}) collective-permute-start(f32[2,256]{1,0:T(2,128)S(1)} %get-tuple-element.213), channel_id=1, source_target_pairs={{0,1},{1,2},{2,3},{3,4},{4,5},{5,6},{6,7},{7,8},{8,9},{9,10},{10,1... | collective-permute-start | bytes 6152 | tf_op jit(solution)/shard_map/while/body/eval_jaxpr/ppermute | solution.py:17
  82.1 9.3 %collective-permute-start.1 = (s32[8]{0:T(128)S(1)}, s32[8]{0:T(128)S(1)}, u32[]{:S(2)}, u32[]{:S(2)}) collective-permute-start(s32[8]{0:T(128)S(1)} %get-tuple-element.215), channel_id=1, source_target_pairs={{0,1},{1,2},{2,3},{3,4},{4,5},{5,6},{6,7},{7,8},{8,9},{9,10},{10,1... | collective-permute-start | bytes 104 | tf_op jit(solution)/shard_map/while/body/eval_jaxpr/ppermute | solution.py:17
  82.1 10.2 %collective-permute-start.3 = (bf16[8,128,128]{2,1,0:T(8,128)(2,1)S(1)}, bf16[8,128,128]{2,1,0:T(8,128)(2,1)S(1)}, u32[]{:S(2)}, u32[]{:S(2)}) collective-permute-start(bf16[8,128,128]{2,1,0:T(8,128)(2,1)S(1)} %get-tuple-element.212), channel_id=1, source_target_pairs={{0,1},{1,2},{2,3},{3,4},{4,5},{5,6},{6,7},{7,8},{8,9},{9,10},{10,1... | collective-permute-start | bytes 786440 | tf_op jit(solution)/shard_map/while/body/eval_jaxpr/ppermute | solution.py:17
  96.8 9.5 %collective-permute-start.4 = (f32[2,256]{1,0:T(2,128)S(1)}, f32[2,256]{1,0:T(2,128)S(1)}, u32[]{:S(2)}, u32[]{:S(2)}) collective-permute-start(f32[2,256]{1,0:T(2,128)S(1)} %get-tuple-element.213), channel_id=1, source_target_pairs={{0,1},{1,2},{2,3},{3,4},{4,5},{5,6},{6,7},{7,8},{8,9},{9,10},{10,1... | collective-permute-start | bytes 6152 | tf_op jit(solution)/shard_map/while/body/eval_jaxpr/ppermute | solution.py:17
  96.9 9.3 %collective-permute-start.1 = (s32[8]{0:T(128)S(1)}, s32[8]{0:T(128)S(1)}, u32[]{:S(2)}, u32[]{:S(2)}) collective-permute-start(s32[8]{0:T(128)S(1)} %get-tuple-element.215), channel_id=1, source_target_pairs={{0,1},{1,2},{2,3},{3,4},{4,5},{5,6},{6,7},{7,8},{8,9},{9,10},{10,1... | collective-permute-start | bytes 104 | tf_op jit(solution)/shard_map/while/body/eval_jaxpr/ppermute | solution.py:17
  96.9 10.2 %collective-permute-start.3 = (bf16[8,128,128]{2,1,0:T(8,128)(2,1)S(1)}, bf16[8,128,128]{2,1,0:T(8,128)(2,1)S(1)}, u32[]{:S(2)}, u32[]{:S(2)}) collective-permute-start(bf16[8,128,128]{2,1,0:T(8,128)(2,1)S(1)} %get-tuple-element.212), channel_id=1, source_target_pairs={{0,1},{1,2},{2,3},{3,4},{4,5},{5,6},{6,7},{7,8},{8,9},{9,10},{10,1... | collective-permute-start | bytes 786440 | tf_op jit(solution)/shard_map/while/body/eval_jaxpr/ppermute | solution.py:17
  97.0 8.5 %collective-permute-start.2 = (s32[1]{0:T(128)}, s32[1]{0:T(128)}, u32[]{:S(2)}, u32[]{:S(2)}) collective-permute-start(s32[1]{0:T(128)} %copy.35), channel_id=1, source_target_pairs={{0,1},{1,2},{2,3},{3,4},{4,5},{5,6},{6,7},{7,8},{8,9},{9,10},{10,1... | collective-permute-start | bytes 20 | tf_op jit(solution)/shard_map/while/body/eval_jaxpr/ppermute | solution.py:17
  111.6 9.5 %collective-permute-start.4 = (f32[2,256]{1,0:T(2,128)S(1)}, f32[2,256]{1,0:T(2,128)S(1)}, u32[]{:S(2)}, u32[]{:S(2)}) collective-permute-start(f32[2,256]{1,0:T(2,128)S(1)} %get-tuple-element.213), channel_id=1, source_target_pairs={{0,1},{1,2},{2,3},{3,4},{4,5},{5,6},{6,7},{7,8},{8,9},{9,10},{10,1... | collective-permute-start | bytes 6152 | tf_op jit(solution)/shard_map/while/body/eval_jaxpr/ppermute | solution.py:17
  111.7 9.3 %collective-permute-start.1 = (s32[8]{0:T(128)S(1)}, s32[8]{0:T(128)S(1)}, u32[]{:S(2)}, u32[]{:S(2)}) collective-permute-start(s32[8]{0:T(128)S(1)} %get-tuple-element.215), channel_id=1, source_target_pairs={{0,1},{1,2},{2,3},{3,4},{4,5},{5,6},{6,7},{7,8},{8,9},{9,10},{10,1... | collective-permute-start | bytes 104 | tf_op jit(solution)/shard_map/while/body/eval_jaxpr/ppermute | solution.py:17
  111.7 10.2 %collective-permute-start.3 = (bf16[8,128,128]{2,1,0:T(8,128)(2,1)S(1)}, bf16[8,128,128]{2,1,0:T(8,128)(2,1)S(1)}, u32[]{:S(2)}, u32[]{:S(2)}) collective-permute-start(bf16[8,128,128]{2,1,0:T(8,128)(2,1)S(1)} %get-tuple-element.212), channel_id=1, source_target_pairs={{0,1},{1,2},{2,3},{3,4},{4,5},{5,6},{6,7},{7,8},{8,9},{9,10},{10,1... | collective-permute-start | bytes 786440 | tf_op jit(solution)/shard_map/while/body/eval_jaxpr/ppermute | solution.py:17
  126.4 9.5 %collective-permute-start.4 = (f32[2,256]{1,0:T(2,128)S(1)}, f32[2,256]{1,0:T(2,128)S(1)}, u32[]{:S(2)}, u32[]{:S(2)}) collective-permute-start(f32[2,256]{1,0:T(2,128)S(1)} %get-tuple-element.213), channel_id=1, source_target_pairs={{0,1},{1,2},{2,3},{3,4},{4,5},{5,6},{6,7},{7,8},{8,9},{9,10},{10,1... | collective-permute-start | bytes 6152 | tf_op jit(solution)/shard_map/while/body/eval_jaxpr/ppermute | solution.py:17
  126.5 9.3 %collective-permute-start.1 = (s32[8]{0:T(128)S(1)}, s32[8]{0:T(128)S(1)}, u32[]{:S(2)}, u32[]{:S(2)}) collective-permute-start(s32[8]{0:T(128)S(1)} %get-tuple-element.215), channel_id=1, source_target_pairs={{0,1},{1,2},{2,3},{3,4},{4,5},{5,6},{6,7},{7,8},{8,9},{9,10},{10,1... | collective-permute-start | bytes 104 | tf_op jit(solution)/shard_map/while/body/eval_jaxpr/ppermute | solution.py:17
  126.6 10.2 %collective-permute-start.3 = (bf16[8,128,128]{2,1,0:T(8,128)(2,1)S(1)}, bf16[8,128,128]{2,1,0:T(8,128)(2,1)S(1)}, u32[]{:S(2)}, u32[]{:S(2)}) collective-permute-start(bf16[8,128,128]{2,1,0:T(8,128)(2,1)S(1)} %get-tuple-element.212), channel_id=1, source_target_pairs={{0,1},{1,2},{2,3},{3,4},{4,5},{5,6},{6,7},{7,8},{8,9},{9,10},{10,1... | collective-permute-start | bytes 786440 | tf_op jit(solution)/shard_map/while/body/eval_jaxpr/ppermute | solution.py:17
  126.6 8.5 %collective-permute-start.2 = (s32[1]{0:T(128)}, s32[1]{0:T(128)}, u32[]{:S(2)}, u32[]{:S(2)}) collective-permute-start(s32[1]{0:T(128)} %copy.35), channel_id=1, source_target_pairs={{0,1},{1,2},{2,3},{3,4},{4,5},{5,6},{6,7},{7,8},{8,9},{9,10},{10,1... | collective-permute-start | bytes 20 | tf_op jit(solution)/shard_map/while/body/eval_jaxpr/ppermute | solution.py:17
  141.2 9.5 %collective-permute-start.4 = (f32[2,256]{1,0:T(2,128)S(1)}, f32[2,256]{1,0:T(2,128)S(1)}, u32[]{:S(2)}, u32[]{:S(2)}) collective-permute-start(f32[2,256]{1,0:T(2,128)S(1)} %get-tuple-element.213), channel_id=1, source_target_pairs={{0,1},{1,2},{2,3},{3,4},{4,5},{5,6},{6,7},{7,8},{8,9},{9,10},{10,1... | collective-permute-start | bytes 6152 | tf_op jit(solution)/shard_map/while/body/eval_jaxpr/ppermute | solution.py:17
  141.3 9.3 %collective-permute-start.1 = (s32[8]{0:T(128)S(1)}, s32[8]{0:T(128)S(1)}, u32[]{:S(2)}, u32[]{:S(2)}) collective-permute-start(s32[8]{0:T(128)S(1)} %get-tuple-element.215), channel_id=1, source_target_pairs={{0,1},{1,2},{2,3},{3,4},{4,5},{5,6},{6,7},{7,8},{8,9},{9,10},{10,1... | collective-permute-start | bytes 104 | tf_op jit(solution)/shard_map/while/body/eval_jaxpr/ppermute | solution.py:17
  141.3 10.2 %collective-permute-start.3 = (bf16[8,128,128]{2,1,0:T(8,128)(2,1)S(1)}, bf16[8,128,128]{2,1,0:T(8,128)(2,1)S(1)}, u32[]{:S(2)}, u32[]{:S(2)}) collective-permute-start(bf16[8,128,128]{2,1,0:T(8,128)(2,1)S(1)} %get-tuple-element.212), channel_id=1, source_target_pairs={{0,1},{1,2},{2,3},{3,4},{4,5},{5,6},{6,7},{7,8},{8,9},{9,10},{10,1... | collective-permute-start | bytes 786440 | tf_op jit(solution)/shard_map/while/body/eval_jaxpr/ppermute | solution.py:17
  156.1 9.5 %collective-permute-start.4 = (f32[2,256]{1,0:T(2,128)S(1)}, f32[2,256]{1,0:T(2,128)S(1)}, u32[]{:S(2)}, u32[]{:S(2)}) collective-permute-start(f32[2,256]{1,0:T(2,128)S(1)} %get-tuple-element.213), channel_id=1, source_target_pairs={{0,1},{1,2},{2,3},{3,4},{4,5},{5,6},{6,7},{7,8},{8,9},{9,10},{10,1... | collective-permute-start | bytes 6152 | tf_op jit(solution)/shard_map/while/body/eval_jaxpr/ppermute | solution.py:17
  156.1 9.3 %collective-permute-start.1 = (s32[8]{0:T(128)S(1)}, s32[8]{0:T(128)S(1)}, u32[]{:S(2)}, u32[]{:S(2)}) collective-permute-start(s32[8]{0:T(128)S(1)} %get-tuple-element.215), channel_id=1, source_target_pairs={{0,1},{1,2},{2,3},{3,4},{4,5},{5,6},{6,7},{7,8},{8,9},{9,10},{10,1... | collective-permute-start | bytes 104 | tf_op jit(solution)/shard_map/while/body/eval_jaxpr/ppermute | solution.py:17
  156.2 10.2 %collective-permute-start.3 = (bf16[8,128,128]{2,1,0:T(8,128)(2,1)S(1)}, bf16[8,128,128]{2,1,0:T(8,128)(2,1)S(1)}, u32[]{:S(2)}, u32[]{:S(2)}) collective-permute-start(bf16[8,128,128]{2,1,0:T(8,128)(2,1)S(1)} %get-tuple-element.212), channel_id=1, source_target_pairs={{0,1},{1,2},{2,3},{3,4},{4,5},{5,6},{6,7},{7,8},{8,9},{9,10},{10,1... | collective-permute-start | bytes 786440 | tf_op jit(solution)/shard_map/while/body/eval_jaxpr/ppermute | solution.py:17
  170.9 9.5 %collective-permute-start.4 = (f32[2,256]{1,0:T(2,128)S(1)}, f32[2,256]{1,0:T(2,128)S(1)}, u32[]{:S(2)}, u32[]{:S(2)}) collective-permute-start(f32[2,256]{1,0:T(2,128)S(1)} %get-tuple-element.213), channel_id=1, source_target_pairs={{0,1},{1,2},{2,3},{3,4},{4,5},{5,6},{6,7},{7,8},{8,9},{9,10},{10,1... | collective-permute-start | bytes 6152 | tf_op jit(solution)/shard_map/while/body/eval_jaxpr/ppermute | solution.py:17
  171.0 9.3 %collective-permute-start.1 = (s32[8]{0:T(128)S(1)}, s32[8]{0:T(128)S(1)}, u32[]{:S(2)}, u32[]{:S(2)}) collective-permute-start(s32[8]{0:T(128)S(1)} %get-tuple-element.215), channel_id=1, source_target_pairs={{0,1},{1,2},{2,3},{3,4},{4,5},{5,6},{6,7},{7,8},{8,9},{9,10},{10,1... | collective-permute-start | bytes 104 | tf_op jit(solution)/shard_map/while/body/eval_jaxpr/ppermute | solution.py:17
  171.0 10.2 %collective-permute-start.3 = (bf16[8,128,128]{2,1,0:T(8,128)(2,1)S(1)}, bf16[8,128,128]{2,1,0:T(8,128)(2,1)S(1)}, u32[]{:S(2)}, u32[]{:S(2)}) collective-permute-start(bf16[8,128,128]{2,1,0:T(8,128)(2,1)S(1)} %get-tuple-element.212), channel_id=1, source_target_pairs={{0,1},{1,2},{2,3},{3,4},{4,5},{5,6},{6,7},{7,8},{8,9},{9,10},{10,1... | collective-permute-start | bytes 786440 | tf_op jit(solution)/shard_map/while/body/eval_jaxpr/ppermute | solution.py:17
  185.7 9.5 %collective-permute-start.4 = (f32[2,256]{1,0:T(2,128)S(1)}, f32[2,256]{1,0:T(2,128)S(1)}, u32[]{:S(2)}, u32[]{:S(2)}) collective-permute-start(f32[2,256]{1,0:T(2,128)S(1)} %get-tuple-element.213), channel_id=1, source_target_pairs={{0,1},{1,2},{2,3},{3,4},{4,5},{5,6},{6,7},{7,8},{8,9},{9,10},{10,1... | collective-permute-start | bytes 6152 | tf_op jit(solution)/shard_map/while/body/eval_jaxpr/ppermute | solution.py:17
  185.8 9.3 %collective-permute-start.1 = (s32[8]{0:T(128)S(1)}, s32[8]{0:T(128)S(1)}, u32[]{:S(2)}, u32[]{:S(2)}) collective-permute-start(s32[8]{0:T(128)S(1)} %get-tuple-element.215), channel_id=1, source_target_pairs={{0,1},{1,2},{2,3},{3,4},{4,5},{5,6},{6,7},{7,8},{8,9},{9,10},{10,1... | collective-permute-start | bytes 104 | tf_op jit(solution)/shard_map/while/body/eval_jaxpr/ppermute | solution.py:17
  185.9 10.2 %collective-permute-start.3 = (bf16[8,128,128]{2,1,0:T(8,128)(2,1)S(1)}, bf16[8,128,128]{2,1,0:T(8,128)(2,1)S(1)}, u32[]{:S(2)}, u32[]{:S(2)}) collective-permute-start(bf16[8,128,128]{2,1,0:T(8,128)(2,1)S(1)} %get-tuple-element.212), channel_id=1, source_target_pairs={{0,1},{1,2},{2,3},{3,4},{4,5},{5,6},{6,7},{7,8},{8,9},{9,10},{10,1... | collective-permute-start | bytes 786440 | tf_op jit(solution)/shard_map/while/body/eval_jaxpr/ppermute | solution.py:17
  200.6 9.5 %collective-permute-start.4 = (f32[2,256]{1,0:T(2,128)S(1)}, f32[2,256]{1,0:T(2,128)S(1)}, u32[]{:S(2)}, u32[]{:S(2)}) collective-permute-start(f32[2,256]{1,0:T(2,128)S(1)} %get-tuple-element.213), channel_id=1, source_target_pairs={{0,1},{1,2},{2,3},{3,4},{4,5},{5,6},{6,7},{7,8},{8,9},{9,10},{10,1... | collective-permute-start | bytes 6152 | tf_op jit(solution)/shard_map/while/body/eval_jaxpr/ppermute | solution.py:17
  200.6 9.3 %collective-permute-start.1 = (s32[8]{0:T(128)S(1)}, s32[8]{0:T(128)S(1)}, u32[]{:S(2)}, u32[]{:S(2)}) collective-permute-start(s32[8]{0:T(128)S(1)} %get-tuple-element.215), channel_id=1, source_target_pairs={{0,1},{1,2},{2,3},{3,4},{4,5},{5,6},{6,7},{7,8},{8,9},{9,10},{10,1... | collective-permute-start | bytes 104 | tf_op jit(solution)/shard_map/while/body/eval_jaxpr/ppermute | solution.py:17
  200.7 10.2 %collective-permute-start.3 = (bf16[8,128,128]{2,1,0:T(8,128)(2,1)S(1)}, bf16[8,128,128]{2,1,0:T(8,128)(2,1)S(1)}, u32[]{:S(2)}, u32[]{:S(2)}) collective-permute-start(bf16[8,128,128]{2,1,0:T(8,128)(2,1)S(1)} %get-tuple-element.212), channel_id=1, source_target_pairs={{0,1},{1,2},{2,3},{3,4},{4,5},{5,6},{6,7},{7,8},{8,9},{9,10},{10,1... | collective-permute-start | bytes 786440 | tf_op jit(solution)/shard_map/while/body/eval_jaxpr/ppermute | solution.py:17
  215.3 9.5 %collective-permute-start.4 = (f32[2,256]{1,0:T(2,128)S(1)}, f32[2,256]{1,0:T(2,128)S(1)}, u32[]{:S(2)}, u32[]{:S(2)}) collective-permute-start(f32[2,256]{1,0:T(2,128)S(1)} %get-tuple-element.213), channel_id=1, source_target_pairs={{0,1},{1,2},{2,3},{3,4},{4,5},{5,6},{6,7},{7,8},{8,9},{9,10},{10,1... | collective-permute-start | bytes 6152 | tf_op jit(solution)/shard_map/while/body/eval_jaxpr/ppermute | solution.py:17
  215.4 9.3 %collective-permute-start.1 = (s32[8]{0:T(128)S(1)}, s32[8]{0:T(128)S(1)}, u32[]{:S(2)}, u32[]{:S(2)}) collective-permute-start(s32[8]{0:T(128)S(1)} %get-tuple-element.215), channel_id=1, source_target_pairs={{0,1},{1,2},{2,3},{3,4},{4,5},{5,6},{6,7},{7,8},{8,9},{9,10},{10,1... | collective-permute-start | bytes 104 | tf_op jit(solution)/shard_map/while/body/eval_jaxpr/ppermute | solution.py:17
  215.4 10.2 %collective-permute-start.3 = (bf16[8,128,128]{2,1,0:T(8,128)(2,1)S(1)}, bf16[8,128,128]{2,1,0:T(8,128)(2,1)S(1)}, u32[]{:S(2)}, u32[]{:S(2)}) collective-permute-start(bf16[8,128,128]{2,1,0:T(8,128)(2,1)S(1)} %get-tuple-element.212), channel_id=1, source_target_pairs={{0,1},{1,2},{2,3},{3,4},{4,5},{5,6},{6,7},{7,8},{8,9},{9,10},{10,1... | collective-permute-start | bytes 786440 | tf_op jit(solution)/shard_map/while/body/eval_jaxpr/ppermute | solution.py:17
  230.1 9.5 %collective-permute-start.4 = (f32[2,256]{1,0:T(2,128)S(1)}, f32[2,256]{1,0:T(2,128)S(1)}, u32[]{:S(2)}, u32[]{:S(2)}) collective-permute-start(f32[2,256]{1,0:T(2,128)S(1)} %get-tuple-element.213), channel_id=1, source_target_pairs={{0,1},{1,2},{2,3},{3,4},{4,5},{5,6},{6,7},{7,8},{8,9},{9,10},{10,1... | collective-permute-start | bytes 6152 | tf_op jit(solution)/shard_map/while/body/eval_jaxpr/ppermute | solution.py:17
  230.2 9.3 %collective-permute-start.1 = (s32[8]{0:T(128)S(1)}, s32[8]{0:T(128)S(1)}, u32[]{:S(2)}, u32[]{:S(2)}) collective-permute-start(s32[8]{0:T(128)S(1)} %get-tuple-element.215), channel_id=1, source_target_pairs={{0,1},{1,2},{2,3},{3,4},{4,5},{5,6},{6,7},{7,8},{8,9},{9,10},{10,1... | collective-permute-start | bytes 104 | tf_op jit(solution)/shard_map/while/body/eval_jaxpr/ppermute | solution.py:17
  230.3 10.2 %collective-permute-start.3 = (bf16[8,128,128]{2,1,0:T(8,128)(2,1)S(1)}, bf16[8,128,128]{2,1,0:T(8,128)(2,1)S(1)}, u32[]{:S(2)}, u32[]{:S(2)}) collective-permute-start(bf16[8,128,128]{2,1,0:T(8,128)(2,1)S(1)} %get-tuple-element.212), channel_id=1, source_target_pairs={{0,1},{1,2},{2,3},{3,4},{4,5},{5,6},{6,7},{7,8},{8,9},{9,10},{10,1... | collective-permute-start | bytes 786440 | tf_op jit(solution)/shard_map/while/body/eval_jaxpr/ppermute | solution.py:17
  (32 other events, 318.8 us)
Sparse Core Ops, SparseCore 0:
  291.5 71.1 reduce-scatter.1
where the time goes:
time: 372 us; the launch traced here: 371 us
  waiting for transfers between devices  168 us (45%)
  other arithmetic  84 us (23%)
  starting transfers between devices  36 us (10%)
  local copies, waits for them, and re-layouts  32 us (9%)
  matrix products  24.5 us (7%)
  between operations  14.2 us (4%)
  loops' own time  12.4 us (3%)
    ppermute x75, waiting for transfers between devices, from_behind(): return lax.ppermute(value, axis, pairs)  97 us
    reduce_scatter x1, waiting for transfers between devices, local(): summed = lax.psum_scatter(running, 'cells', scatter_dimension=0, tiled=True)  71.3 us
    scatter-add x16, other arithmetic, absorb(): return accumulator.at[week_index, row_index].add(products)  53.9 us
    ppermute x75, starting transfers between devices, from_behind(): return lax.ppermute(value, axis, pairs)  36 us
    dot_general x1, matrix products, local(): jnp.einsum('wv,vrim->wrim', time_cov, accumulator, precision=lax.Precisio...  15.3 us
    another operation x1, loops' own time, local(): lax.fori_loop(0, lax.axis_size('cells') - 1, hop, cycle_state)[0]  12.4 us
    gather x16, local copies, waits for them, and re-layouts, absorb(): jnp.take(covar.reshape(cell_count, per_week, tile_edge), cell_block, axis=1)  10.4 us
    lt x15, other arithmetic, absorb(): live = jnp.arange(slot_count, dtype=jnp.int32) < live_count  10.1 us
  transfers between devices with their start and end apart: 76, of which 16 were waited for; matrix products, arithmetic and copies ran while one was open for 6% of the time, Pallas kernels for 0%

commit v1 on v0

v1 whole, which is shorter than its diff:
```python
import functools

import jax
import jax.numpy as jnp
from jax import lax
from jax.experimental import pallas as pl
from jax.experimental.pallas import tpu as pltpu
from jax.sharding import PartitionSpec as P

WEEKS = 8
OBS = 1024
TILE = 128
SPACE_RANGE = 1.0
TIME_RANGE = 3.0
CHUNKS = 2
VMEM_BYTES = 56 * 1024 * 1024


def place(lines):
    me = lax.axis_index("cells")
    chip = me // 2
    return me, me % 2, chip, chip % lines, chip // lines


def remote(src, dst, send, recv, target):
    return pltpu.make_async_remote_copy(
        src_ref=src,
        dst_ref=dst,
        send_sem=send,
        recv_sem=recv,
        device_id={"cells": target},
        device_id_type=pl.DeviceIdType.MESH,
    )


def signal(sem, target):
    pl.semaphore_signal(
        sem, inc=1, device_id={"cells": target}, device_id_type=pl.DeviceIdType.MESH
    )


def gather_kernel(
    chips, lines, own, packet, tiles, home_tiles, covar, meta,
    packets, home_pos, pkt_send, pkt_recv, sib_send, sib_recv, hop_send, hop_recv,
):
    depth = chips // lines
    me, core, chip, y, z = place(lines)
    sibling = me + 1 - 2 * core
    slots = own.shape[0]
    part = slots // CHUNKS
    cells = home_pos.shape[1] // 2
    per_dev = cells // TILE

    barrier = pltpu.get_barrier_semaphore()
    for k in range(1, chips):
        signal(barrier, lax.rem(chip + k, chips) * 2 + core)
    signal(barrier, sibling)
    pl.semaphore_wait(barrier, chips)

    pkt_copies = [remote(packet, packets.at[chips], pkt_send.at[0], pkt_recv.at[0], sibling)]
    for k in range(1, chips):
        pkt_copies.append(
            remote(packet, packets.at[chip], pkt_send.at[k], pkt_recv.at[k],
                   lax.rem(chip + k, chips) * 2 + core)
        )
    for copy in pkt_copies:
        copy.start()

    def block(q, ch):
        return tiles.at[pl.ds(q * slots + ch * part, part)]

    sends = []

    def send(cond, kind, step, q, ch, target, first):
        source = own.at[pl.ds(ch * part, part)] if first else block(q, ch)
        copy = remote(source, block(q, ch), hop_send.at[kind, step, ch],
                      hop_recv.at[q * CHUNKS + ch], target)
        sends.append((cond, copy))
        if cond is None:
            copy.start()
        else:
            pl.when(cond)(copy.start)

    def arrive(q, ch):
        remote(block(q, ch), block(q, ch), hop_send.at[0, 0, 0],
               hop_recv.at[q * CHUNKS + ch], sibling).wait_recv()

    above = me + 2 * lines
    below = me - 2 * lines
    across = me + 2 - 4 * y
    for ch in range(CHUNKS):
        send(z < depth - 1, 0, 0, chip, ch, above, True)
        send(z > 0, 1, 0, chip, ch, below, True)
        if lines == 2:
            send(None, 2, 0, chip, ch, across, True)
    sib_copy = remote(own, home_tiles.at[pl.ds(core * slots, slots)], sib_send, sib_recv, sibling)
    sib_copy.start()
    tiles[pl.ds(chip * slots, slots)] = own[...]
    home_tiles[pl.ds(core * slots, slots)] = own[...]
    packets[chip] = packet[...]

    for copy in pkt_copies:
        copy.wait()

    mine = packet[...]
    other = packets[chips]
    is_first = (core == 0).astype(jnp.float32)
    pair = (mine * is_first + other * (1.0 - is_first), other * is_first + mine * (1.0 - is_first))
    for q in range(chips):
        meta[q] = packets[q].astype(jnp.int32)
    for j in range(2):
        meta[chips + j] = pair[j].astype(jnp.int32)
        columns = jnp.transpose(pair[j])
        for b in range(per_dev):
            rows = pl.ds(j * cells + b * TILE, TILE)
            for axis in range(2):
                col = columns[:, axis * per_dev + b : axis * per_dev + b + 1]
                home_pos[axis, rows, :] = jnp.broadcast_to(col, (TILE, TILE))

    step_rows = 64

    @pl.loop(0, chips)
    def _(q):
        for b in range(per_dev):
            east = packets[q, b : b + 1, :]
            north = packets[q, per_dev + b : per_dev + b + 1, :]

            @pl.loop(0, home_pos.shape[1] // step_rows)
            def _(i):
                rows = pl.ds(i * step_rows, step_rows)
                dx = home_pos[0, rows, :] - east
                dy = home_pos[1, rows, :] - north
                covar[q * per_dev + b, rows, :] = jnp.exp(
                    -jnp.sqrt(dx * dx + dy * dy) / SPACE_RANGE
                ).astype(jnp.bfloat16)

    for d in range(1, depth):
        for ch in range(CHUNKS):
            def from_below(d=d, ch=ch):
                arrive((z - d) * lines + y, ch)

            def from_above(d=d, ch=ch):
                arrive((z + d) * lines + y, ch)

            q_low = (z - d) * lines + y
            q_high = (z + d) * lines + y
            pl.when(z >= d)(from_below)
            if d < depth - 1:
                send((z >= d) & (z < depth - 1), 0, d, q_low, ch, above, False)
            if lines == 2:
                send(z >= d, 2, d, q_low, ch, across, False)
            pl.when(z + d < depth)(from_above)
            if d < depth - 1:
                send((z + d < depth) & (z > 0), 1, d, q_high, ch, below, False)
            if lines == 2:
                send(z + d < depth, 3, d, q_high, ch, across, False)
    if lines == 2:
        for zz in range(depth):
            for ch in range(CHUNKS):
                arrive(zz * lines + 1 - y, ch)
    for cond, copy in sends:
        if cond is None:
            copy.wait_send()
        else:
            pl.when(cond)(copy.wait_send)
    sib_copy.wait()


def spread_kernel(chips, meta, tiles, home_tiles, covar, out, acc, weighted):
    slots = tiles.shape[0] // chips
    homes = covar.shape[1]
    cells = homes // 2
    per_dev = cells // TILE
    row_tiles = OBS // TILE

    @pl.loop(0, WEEKS * row_tiles)
    def _(i):
        acc[i] = jnp.zeros((homes, TILE), jnp.float32)

    def place_of(d, s):
        col = meta[d, 4, slots + s]
        return meta[d, 4, s], col // per_dev, col % per_dev

    @pl.loop(0, chips)
    def _(q):
        @pl.loop(0, meta[q, 4, 2 * slots])
        def _(s):
            row, week, b = place_of(q, s)
            strip = covar[q * per_dev + b]
            product = lax.dot_general(
                strip, tiles[q * slots + s], (((1,), (1,)), ((), ())),
                preferred_element_type=jnp.float32,
            )
            acc[week * row_tiles + row] += product

    decay = jnp.exp(jnp.float32(-1.0 / TIME_RANGE))
    step_rows = 16
    for r in range(row_tiles):
        @pl.loop(0, homes // step_rows)
        def _(i):
            rows = pl.ds(i * step_rows, step_rows)
            spread = [acc[w * row_tiles + r, rows, :] for w in range(WEEKS)]
            ahead = [spread[0]]
            for w in range(1, WEEKS):
                ahead.append(spread[w] + decay * ahead[-1])
            back = None
            for w in reversed(range(WEEKS)):
                total = ahead[w] if back is None else ahead[w] + back
                weighted[w, rows, r * TILE : (r + 1) * TILE] = total.astype(jnp.bfloat16)
                back = decay * (spread[w] if back is None else spread[w] + back)

    out[...] = jnp.zeros_like(out)
    for j in range(2):
        @pl.loop(0, meta[chips + j, 4, 2 * slots])
        def _(s):
            row, week, b = place_of(chips + j, s)
            slab = weighted[week, pl.ds(pl.multiple_of(j * cells + b * TILE, TILE), TILE), :]
            product = jnp.dot(
                home_tiles[j * slots + s], slab, preferred_element_type=jnp.float32
            )
            out[pl.ds(pl.multiple_of(row * TILE, TILE), TILE), :] += product


def reduce_kernel(
    chips, lines, partial, obs, out, sib, y_out, y_in, z_out, z_in,
    sib_send, sib_recv, y_send, y_recv, z_send, z_recv,
):
    depth = chips // lines
    me, core, chip, y, z = place(lines)
    sibling = me + 1 - 2 * core
    rows = out.shape[0]
    above = me + 2 * lines
    below = me - 2 * lines
    across = me + 2 - 4 * y
    up_ok = z < depth - 1
    down_ok = z > 0

    barrier = pltpu.get_barrier_semaphore()
    signal(barrier, sibling)
    if lines == 2:
        signal(barrier, across)
    pl.when(up_ok)(lambda: signal(barrier, above))
    pl.when(down_ok)(lambda: signal(barrier, below))
    pl.semaphore_wait(barrier, lines + up_ok.astype(jnp.int32) + down_ok.astype(jnp.int32))

    upper = (z >= depth // 2).astype(jnp.int32)

    def order(j):
        if j == depth - 1:
            return z
        high = depth - 1 - j
        high = high - (high <= z).astype(jnp.int32)
        low = j + (j >= z).astype(jnp.int32)
        return upper * low + (1 - upper) * high

    def slab(q, k):
        return partial.at[pl.ds(pl.multiple_of((q * 2 + k) * rows, 8), rows)]

    def sib_copy(q):
        return remote(slab(q, 1 - core), sib.at[q], sib_send.at[q], sib_recv.at[q], sibling)

    columns = list(reversed(range(lines)))
    for line in columns:
        for j in range(depth):
            sib_copy(order(j) * lines + (y + line) % lines).start()

    def chip_sum(q):
        sib_copy(q).wait_recv()
        return slab(q, core)[...] + sib[q]

    if lines == 2:
        for j in range(depth):
            c = order(j)
            y_out[c] = chip_sum(c * lines + 1 - y).astype(jnp.bfloat16)
            remote(y_out.at[c], y_in.at[c], y_send.at[c], y_recv.at[c], across).start()

    def up_copy(c):
        return remote(z_out.at[c], z_in.at[0, c], z_send.at[c], z_recv.at[0, c], above)

    def down_copy(c):
        return remote(z_out.at[c], z_in.at[1, c], z_send.at[c], z_recv.at[1, c], below)

    for j in range(depth - 1):
        c = order(j)
        total = chip_sum(c * lines + y)
        if lines == 2:
            remote(y_out.at[c], y_in.at[c], y_send.at[c], y_recv.at[c], across).wait_recv()
            total = total + y_in[c].astype(jnp.float32)
        out[...] = total

        @pl.when((c > z) & down_ok)
        def _():
            up_copy(c).wait_recv()
            out[...] += z_in[0, c].astype(jnp.float32)

        @pl.when((c < z) & up_ok)
        def _():
            down_copy(c).wait_recv()
            out[...] += z_in[1, c].astype(jnp.float32)

        z_out[c] = out[...].astype(jnp.bfloat16)

        @pl.when(c > z)
        def _():
            up_copy(c).start()

        @pl.when(c < z)
        def _():
            down_copy(c).start()

    total = chip_sum(chip)
    if lines == 2:
        remote(y_out.at[z], y_in.at[z], y_send.at[z], y_recv.at[z], across).wait_recv()
        total = total + y_in[z].astype(jnp.float32)
    shape = (rows, rows)
    eye = lax.broadcasted_iota(jnp.int32, shape, 0) == lax.broadcasted_iota(jnp.int32, shape, 1)
    errors = jnp.sum(
        jnp.where(eye, jnp.broadcast_to(obs[...], shape), 0.0), axis=1, keepdims=True
    )
    hit = lax.broadcasted_iota(jnp.int32, out.shape, 1) == (
        me * rows + lax.broadcasted_iota(jnp.int32, out.shape, 0)
    )
    out[...] = total + jnp.where(hit, jnp.broadcast_to(errors, out.shape), 0.0)

    @pl.when(down_ok)
    def _():
        up_copy(z).wait_recv()
        out[...] += z_in[0, z].astype(jnp.float32)

    @pl.when(up_ok)
    def _():
        down_copy(z).wait_recv()
        out[...] += z_in[1, z].astype(jnp.float32)

    for q in range(chips):
        sib_copy(q).wait_send()
    for c in range(depth):
        if lines == 2:
            remote(y_out.at[c], y_in.at[c], y_send.at[c], y_recv.at[c], across).wait_send()
        pl.when(c != z)(lambda c=c: up_copy(c).wait_send())


def local(footprints, tile_rows, tile_cols, tile_counts, coords, obs_error):
    count = lax.axis_size("cells")
    chips = count // 2
    lines = 2 if chips == 8 else 1
    depth = chips // lines
    slots = footprints.shape[0]
    cells = coords.shape[1]
    per_dev = cells // TILE
    rows = OBS // count
    vmem = pl.BlockSpec(memory_space=pltpu.VMEM)
    smem = pl.BlockSpec(memory_space=pltpu.SMEM)
    dma = pltpu.SemaphoreType.DMA

    places = jnp.concatenate([tile_rows, tile_cols, tile_counts]).astype(jnp.float32)
    places = jnp.pad(places, (0, TILE - places.shape[0]))
    packet = jnp.concatenate([coords.reshape(2 * per_dev, TILE), places[None, :]], axis=0)
    packet = jnp.pad(packet, ((0, 8 - packet.shape[0]), (0, 0)))

    tiles, home_tiles, covar, meta = pl.pallas_call(
        functools.partial(gather_kernel, chips, lines),
        out_shape=(
            jax.ShapeDtypeStruct((chips * slots, TILE, TILE), jnp.bfloat16),
            jax.ShapeDtypeStruct((2 * slots, TILE, TILE), jnp.bfloat16),
            jax.ShapeDtypeStruct((chips * per_dev, 2 * cells, TILE), jnp.bfloat16),
            jax.ShapeDtypeStruct((chips + 2, 8, TILE), jnp.int32),
        ),
        in_specs=[vmem] * 2,
        out_specs=(vmem,) * 4,
        scratch_shapes=[
            pltpu.VMEM((chips + 1, 8, TILE), jnp.float32),
            pltpu.VMEM((2, 2 * cells, TILE), jnp.float32),
            dma((chips,)),
            dma((chips,)),
            dma,
            dma,
            dma((4, depth, CHUNKS)),
            dma((chips * CHUNKS,)),
        ],
        compiler_params=pltpu.CompilerParams(
            collective_id=0, has_side_effects=True, vmem_limit_bytes=VMEM_BYTES
        ),
        name="gather",
    )(footprints, packet)

    partial = pl.pallas_call(
        functools.partial(spread_kernel, chips),
        out_shape=jax.ShapeDtypeStruct((OBS, OBS), jnp.float32),
        in_specs=[smem, vmem, vmem, vmem],
        out_specs=vmem,
        scratch_shapes=[
            pltpu.VMEM((WEEKS * OBS // TILE, 2 * cells, TILE), jnp.float32),
            pltpu.VMEM((WEEKS, 2 * cells, OBS), jnp.bfloat16),
        ],
        compiler_params=pltpu.CompilerParams(vmem_limit_bytes=VMEM_BYTES),
        name="spread",
    )(meta, tiles, home_tiles, covar)

    return pl.pallas_call(
        functools.partial(reduce_kernel, chips, lines),
        out_shape=jax.ShapeDtypeStruct((rows, OBS), jnp.float32),
        in_specs=[vmem] * 2,
        out_specs=vmem,
        scratch_shapes=[
            pltpu.VMEM((chips, rows, OBS), jnp.float32),
            pltpu.VMEM((depth, rows, OBS), jnp.bfloat16),
            pltpu.VMEM((depth, rows, OBS), jnp.bfloat16),
            pltpu.VMEM((depth, rows, OBS), jnp.bfloat16),
            pltpu.VMEM((2, depth, rows, OBS), jnp.bfloat16),
            dma((chips,)),
            dma((chips,)),
            dma((depth,)),
            dma((depth,)),
            dma((depth,)),
            dma((2, depth)),
        ],
        compiler_params=pltpu.CompilerParams(
            collective_id=1, has_side_effects=True, vmem_limit_bytes=VMEM_BYTES
        ),
        name="reduce",
    )(partial, obs_error.reshape(1, rows))


def solution(mesh):
    placed = (
        P(("groups", "cells"), None, None),
        P(("groups", "cells")),
        P(("groups", "cells")),
        P(("groups", "cells")),
        P(None, ("groups", "cells")),
        P(("groups", "cells")),
    )
    return jax.shard_map(
        local, mesh=mesh, in_specs=placed, out_specs=P(("groups", "cells"), None), check_vma=False
    )
```

time: 372 us -> 84.3 us (0.23)
  waiting for transfers between devices: 168 us -> 0 us
  other arithmetic: 84 us -> 1.35 us
  Pallas kernels: 0 us -> 80 us
  starting transfers between devices: 36 us -> 0 us
  local copies, waits for them, and re-layouts: 32 us -> 2.37 us
  matrix products: 24.5 us -> 0 us
  between operations: 14.2 us -> 0.67 us
  loops' own time: 12.4 us -> 0 us
    ppermute x75 -> x0, waiting for transfers between devices: 97 us -> none  [from_behind(): return lax.ppermute(value, axis, pairs)]
    pallas_call x0 -> x3, Pallas kernels: none -> 80 us  [the longest x1 34.3 us: local(): pl.pallas_call(functools.partial(gather_kernel, chips, lines), out_shape=...]
    reduce_scatter x1 -> x0, waiting for transfers between devices: 71.3 us -> none  [local(): summed = lax.psum_scatter(running, 'cells', scatter_dimension=0, tiled=True)]
    scatter-add x17 -> x0, other arithmetic: 63.2 us -> none  [the longest x16 53.9 us: absorb(): return accumulator.at[week_index, row_index].add(products)]
    ppermute x75 -> x0, starting transfers between devices: 36 us -> none  [from_behind(): return lax.ppermute(value, axis, pairs)]
    dot_general x18 -> x0, matrix products: 24.5 us -> none  [the longest x1 15.3 us: local(): jnp.einsum('wv,vrim->wrim', time_cov, accumulator, precision=lax.Precisio...]
    gather x17 -> x0, local copies, waits for them, and re-layouts: 13.5 us -> none  [the longest x16 10.4 us: absorb(): jnp.take(covar.reshape(cell_count, per_week, tile_edge), cell_block, axis=1)]
    another operation x1 -> x0, loops' own time: 12.4 us -> none  [local(): lax.fori_loop(0, lax.axis_size('cells') - 1, hop, cycle_state)[0]]
  transfers between devices with their start and end apart: 76 -> 0, of which waited for: 16 -> 0; matrix products, arithmetic and copies ran while one was open for 6% -> 0% of each run, Pallas kernels for 0% -> 0%
where the time goes in v1:
time: 84.3 us; the launch traced here: 84.4 us
  Pallas kernels  80 us (95%)
  local copies, waits for them, and re-layouts  2.37 us (3%)
  other arithmetic  1.35 us (2%)
    pallas_call x1, Pallas kernels, local(): pl.pallas_call(functools.partial(gather_kernel, chips, lines), out_shape=...  34.3 us
    pallas_call x1, Pallas kernels, local(): pl.pallas_call(functools.partial(reduce_kernel, chips, lines), out_shape=...  24.2 us
    pallas_call x1, Pallas kernels, local(): pl.pallas_call(functools.partial(spread_kernel, chips), out_shape=jax.Sha...  21.6 us

profile of v1, /device:TPU:0, one launch (start us, length us, event | category | flops | bytes accessed | tf_op | source)
XLA Modules:
  0.0 84.4 jit_solution(1355357617767864050)
XLA Ops:
  0.7 0.8 add_convert_fusion
  1.4 0.7 reshape.6
  2.1 0.6 select_maximum_fusion.packet
  2.7 34.3 %gather.1 = (bf16[64,128,128]{2,1,0:T(8,128)(2,1)}, bf16[16,128,128]{2,1,0:T(8,128)(2,1)}, bf16[16,512,128]{2,1,0:T(8,128)(2,1)}, s32[10,8,128]{2,1,0:T(8,128)}) custom-call(bf16[8,128,128]{2,1,0:T(8,128)(2,1)} %own.1, f32[8,128]{1,0:T(8,128)} %select_maximum_fusion.packet), custom_call_target="tpu_custom_call" | custom-call | tf_op jit(solution)/shard_map/gather/pallas_call | solution.py:361
  37.0 21.6 %spread.1.partial = f32[1024,1024]{1,0:T(8,128)} custom-call(s32[10,8,128]{2,1,0:T(8,128)} %get-tuple-element.9.meta, bf16[64,128,128]{2,1,0:T(8,128)(2,1)} %get-tuple-element.10.tiles, bf16[16,128,128]{2,1,0:T(8,128)(2,1)} %get-tuple-element.11.home_tiles, bf16[16,512,128]{2,1,0:T(8,128)(2,1)} %get-tuple-element.12.covar), custom_call_target="tpu_custom_call" | custom-call | tf_op jit(solution)/shard_map/spread/pallas_call | solution.py:387
  58.5 24.2 %reduce.1 = f32[64,1024]{1,0:T(8,128)} custom-call(f32[1024,1024]{1,0:T(8,128)} %spread.1.partial, f32[1,64]{1,0:T(1,128)} %bitcast.3), custom_call_target="tpu_custom_call" | custom-call | tf_op jit(solution)/shard_map/reduce/pallas_call | solution.py:400
  82.7 1.7 %copy.9 = f32[64,1024]{1,0:T(8,128)} copy(f32[64,1024]{1,0:T(8,128)} %reduce.1) | data formatting | bytes 524288
  (1 shorter events, 0.0 us)

commit v2 on v1

--- a/solution.py
+++ b/solution.py
@@ -39,9 +39,10 @@
     )
 
 
-def gather_kernel(
-    chips, lines, own, packet, tiles, home_tiles, covar, meta,
-    packets, home_pos, pkt_send, pkt_recv, sib_send, sib_recv, hop_send, hop_recv,
+def gather_phase(
+    chips, lines, own, packet, info, tiles, home_tiles, covar,
+    packets, infos, home_pos, pkt_send, pkt_recv, sib_send, sib_recv, hop_send, hop_recv,
+    on_places, on_block=None,
 ):
     depth = chips // lines
     me, core, chip, y, z = place(lines)
@@ -57,12 +58,16 @@
     signal(barrier, sibling)
     pl.semaphore_wait(barrier, chips)
 
-    pkt_copies = [remote(packet, packets.at[chips], pkt_send.at[0], pkt_recv.at[0], sibling)]
-    for k in range(1, chips):
+    pkt_copies = []
+    for i, (src, dst) in enumerate(((packet, packets), (info, infos))):
         pkt_copies.append(
-            remote(packet, packets.at[chip], pkt_send.at[k], pkt_recv.at[k],
-                   lax.rem(chip + k, chips) * 2 + core)
+            remote(src, dst.at[chips], pkt_send.at[i, 0], pkt_recv.at[i, 0], sibling)
         )
+        for k in range(1, chips):
+            pkt_copies.append(
+                remote(src, dst.at[chip], pkt_send.at[i, k], pkt_recv.at[i, k],
+                       lax.rem(chip + k, chips) * 2 + core)
+            )
     for copy in pkt_copies:
         copy.start()
 
@@ -98,6 +103,7 @@
     tiles[pl.ds(chip * slots, slots)] = own[...]
     home_tiles[pl.ds(core * slots, slots)] = own[...]
     packets[chip] = packet[...]
+    infos[chip] = info[...]
 
     for copy in pkt_copies:
         copy.wait()
@@ -106,10 +112,11 @@
     other = packets[chips]
     is_first = (core == 0).astype(jnp.float32)
     pair = (mine * is_first + other * (1.0 - is_first), other * is_first + mine * (1.0 - is_first))
-    for q in range(chips):
-        meta[q] = packets[q].astype(jnp.int32)
+    first = jnp.broadcast_to(core == 0, info.shape)
+    on_places((
+        jnp.where(first, info[...], infos[chips]), jnp.where(first, infos[chips], info[...])
+    ))
     for j in range(2):
-        meta[chips + j] = pair[j].astype(jnp.int32)
         columns = jnp.transpose(pair[j])
         for b in range(per_dev):
             rows = pl.ds(j * cells + b * TILE, TILE)
@@ -133,6 +140,26 @@
                 covar[q * per_dev + b, rows, :] = jnp.exp(
                     -jnp.sqrt(dx * dx + dy * dy) / SPACE_RANGE
                 ).astype(jnp.bfloat16)
+
+    def done(q, ch):
+        if on_block is not None:
+            on_block(q, ch)
+
+    def from_across(d, ch):
+        def low():
+            arrive((z - d) * lines + 1 - y, ch)
+            done((z - d) * lines + 1 - y, ch)
+
+        def high():
+            arrive((z + d) * lines + 1 - y, ch)
+            done((z + d) * lines + 1 - y, ch)
+
+        pl.when(z >= d)(low)
+        if d > 0:
+            pl.when(z + d < depth)(high)
+
+    for ch in range(CHUNKS):
+        done(chip, ch)
 
     for d in range(1, depth):
         for ch in range(CHUNKS):
@@ -154,10 +181,16 @@
                 send((z + d < depth) & (z > 0), 1, d, q_high, ch, below, False)
             if lines == 2:
                 send(z + d < depth, 3, d, q_high, ch, across, False)
+        for ch in range(CHUNKS):
+            if on_block is not None:
+                pl.when(z >= d)(lambda: on_block((z - d) * lines + y, ch))
+                pl.when(z + d < depth)(lambda: on_block((z + d) * lines + y, ch))
+        if lines == 2:
+            for ch in range(CHUNKS):
+                from_across(d - 1, ch)
     if lines == 2:
-        for zz in range(depth):
-            for ch in range(CHUNKS):
-                arrive(zz * lines + 1 - y, ch)
+        for ch in range(CHUNKS):
+            from_across(depth - 1, ch)
     for cond, copy in sends:
         if cond is None:
             copy.wait_send()
@@ -166,6 +199,23 @@
     sib_copy.wait()
 
 
+def gather_kernel(
+    chips, lines, own, packet, info, tiles, home_tiles, covar, meta,
+    packets, infos, home_pos, pkt_send, pkt_recv, sib_send, sib_recv, hop_send, hop_recv,
+):
+    def on_places(pair):
+        for q in range(chips):
+            meta[q] = infos[q]
+        for j in range(2):
+            meta[chips + j] = pair[j]
+
+    gather_phase(
+        chips, lines, own, packet, info, tiles, home_tiles, covar,
+        packets, infos, home_pos, pkt_send, pkt_recv, sib_send, sib_recv, hop_send, hop_recv,
+        on_places,
+    )
+
+
 def spread_kernel(chips, meta, tiles, home_tiles, covar, out, acc, weighted):
     slots = tiles.shape[0] // chips
     homes = covar.shape[1]
@@ -178,12 +228,12 @@
         acc[i] = jnp.zeros((homes, TILE), jnp.float32)
 
     def place_of(d, s):
-        col = meta[d, 4, slots + s]
-        return meta[d, 4, s], col // per_dev, col % per_dev
+        col = meta[d, 0, slots + s]
+        return meta[d, 0, s], col // per_dev, col % per_dev
 
     @pl.loop(0, chips)
     def _(q):
-        @pl.loop(0, meta[q, 4, 2 * slots])
+        @pl.loop(0, meta[q, 0, 2 * slots])
         def _(s):
             row, week, b = place_of(q, s)
             strip = covar[q * per_dev + b]
@@ -211,7 +261,7 @@
 
     out[...] = jnp.zeros_like(out)
     for j in range(2):
-        @pl.loop(0, meta[chips + j, 4, 2 * slots])
+        @pl.loop(0, meta[chips + j, 0, 2 * slots])
         def _(s):
             row, week, b = place_of(chips + j, s)
             slab = weighted[week, pl.ds(pl.multiple_of(j * cells + b * TILE, TILE), TILE), :]
@@ -221,9 +271,9 @@
             out[pl.ds(pl.multiple_of(row * TILE, TILE), TILE), :] += product
 
 
-def reduce_kernel(
-    chips, lines, partial, obs, out, sib, y_out, y_in, z_out, z_in,
-    sib_send, sib_recv, y_send, y_recv, z_send, z_recv,
+def reduce_phase(
+    chips, lines, obs, out, sib, y_out, y_in, z_out, z_in,
+    sib_send, sib_recv, y_send, y_recv, z_send, z_recv, outgoing, mine,
 ):
     depth = chips // lines
     me, core, chip, y, z = place(lines)
@@ -235,14 +285,6 @@
     up_ok = z < depth - 1
     down_ok = z > 0
 
-    barrier = pltpu.get_barrier_semaphore()
-    signal(barrier, sibling)
-    if lines == 2:
-        signal(barrier, across)
-    pl.when(up_ok)(lambda: signal(barrier, above))
-    pl.when(down_ok)(lambda: signal(barrier, below))
-    pl.semaphore_wait(barrier, lines + up_ok.astype(jnp.int32) + down_ok.astype(jnp.int32))
-
     upper = (z >= depth // 2).astype(jnp.int32)
 
     def order(j):
@@ -253,11 +295,8 @@
         low = j + (j >= z).astype(jnp.int32)
         return upper * low + (1 - upper) * high
 
-    def slab(q, k):
-        return partial.at[pl.ds(pl.multiple_of((q * 2 + k) * rows, 8), rows)]
-
     def sib_copy(q):
-        return remote(slab(q, 1 - core), sib.at[q], sib_send.at[q], sib_recv.at[q], sibling)
+        return remote(outgoing(q), sib.at[q], sib_send.at[q], sib_recv.at[q], sibling)
 
     columns = list(reversed(range(lines)))
     for line in columns:
@@ -266,7 +305,7 @@
 
     def chip_sum(q):
         sib_copy(q).wait_recv()
-        return slab(q, core)[...] + sib[q]
+        return mine(q) + sib[q]
 
     if lines == 2:
         for j in range(depth):
@@ -338,6 +377,187 @@
         if lines == 2:
             remote(y_out.at[c], y_in.at[c], y_send.at[c], y_recv.at[c], across).wait_send()
         pl.when(c != z)(lambda c=c: up_copy(c).wait_send())
+
+
+def reduce_kernel(chips, lines, partial, obs, out, *scratch):
+    depth = chips // lines
+    me, core, chip, y, z = place(lines)
+    rows = out.shape[0]
+    above = me + 2 * lines
+    below = me - 2 * lines
+    up_ok = z < depth - 1
+    down_ok = z > 0
+    sibling = me + 1 - 2 * core
+    across = me + 2 - 4 * y
+
+    barrier = pltpu.get_barrier_semaphore()
+    signal(barrier, sibling)
+    if lines == 2:
+        signal(barrier, across)
+    pl.when(up_ok)(lambda: signal(barrier, above))
+    pl.when(down_ok)(lambda: signal(barrier, below))
+    pl.semaphore_wait(barrier, lines + up_ok.astype(jnp.int32) + down_ok.astype(jnp.int32))
+
+    def slab(q, k):
+        return partial.at[pl.ds(pl.multiple_of((q * 2 + k) * rows, 8), rows)]
+
+    reduce_phase(
+        chips, lines, obs, out, *scratch,
+        lambda q: slab(q, 1 - core), lambda q: slab(q, core)[...],
+    )
+
+
+def sort_tables(key):
+    square = (TILE, TILE)
+    of_lane = jnp.broadcast_to(key, square)
+    of_row = jnp.transpose(of_lane)
+    row = lax.broadcasted_iota(jnp.int32, square, 0)
+    lane = lax.broadcasted_iota(jnp.int32, square, 1)
+
+    def count(hits):
+        return jnp.sum(jnp.where(hits, 1, 0), axis=0, keepdims=True)
+
+    same_before = (of_row == of_lane) & (row < lane)
+    rank = count((of_row < of_lane) | same_before)
+    repeat = jnp.where(count(same_before) > 0, 1, 0)
+    here = jnp.transpose(jnp.broadcast_to(rank, square)) == lane
+
+    def ordered(values):
+        column = jnp.transpose(jnp.broadcast_to(values, square))
+        return jnp.sum(jnp.where(here, column, 0), axis=0, keepdims=True)
+
+    perm = ordered(lane[0:1, :])
+    held = count(of_row == lane)
+    end = count(of_row <= lane) - 1
+    return ordered, perm, ordered(repeat), end, held
+
+
+def fused_kernel(
+    chips, lines, own, packet, info, obs, out,
+    tiles, home_tiles, covar, products, runs, weighted, home_runs, sib_out,
+    places, whole_tab, share_tab, whole_s, share_s, tab_sem,
+    packets, infos, home_pos, pkt_send, pkt_recv, sib_send, sib_recv, hop_send, hop_recv,
+    sib, y_out, y_in, z_out, z_in, ex_send, ex_recv, y_send, y_recv, z_send, z_recv,
+):
+    slots = own.shape[0]
+    part = slots // CHUNKS
+    total = chips * slots
+    homes = home_pos.shape[1]
+    cells = homes // 2
+    per_dev = cells // TILE
+    row_tiles = OBS // TILE
+    rows = out.shape[0]
+    core = lax.axis_index("cells") % 2
+
+    def places_of(values):
+        n = len(values) * slots
+        places[...] = jnp.zeros((TILE, TILE), jnp.int32)
+        for i, value in enumerate(values):
+            places[i * slots : (i + 1) * slots, :] = jnp.broadcast_to(
+                value[0:1, :], (slots, TILE)
+            )
+        known = jnp.transpose(places[...])
+        row = lax.broadcasted_iota(jnp.int32, (TILE, TILE), 0)
+        lane = lax.broadcasted_iota(jnp.int32, (TILE, TILE), 1)
+        slot = lane % slots
+
+        def pick(at):
+            return jnp.sum(jnp.where(row == at, known, 0), axis=0, keepdims=True)
+
+        row_tile, col_tile, count = pick(slot), pick(slots + slot), pick(2 * slots)
+        live = (slot[0:1, :] < count) & (lane[0:1, :] < n)
+        week = lax.shift_right_logical(col_tile, jnp.full_like(col_tile, per_dev // 2))
+        return row_tile, week, col_tile - per_dev * week, live
+
+    def table(row, values):
+        whole_tab[row : row + 1, :] = values
+
+    def on_places(pair):
+        row_tile, week, cell_block, live = places_of([infos[q] for q in range(chips)])
+        key = jnp.where(live, row_tile * WEEKS + week, WEEKS * row_tiles)
+        _, perm, keep, end, held = sort_tables(key)
+        table(0, perm)
+        table(1, jnp.where(held > 0, end, total))
+        table(2, cell_block)
+        share_tab[0:1, :] = keep.astype(jnp.float32)
+        row_tile, week, cell_block, live = places_of(pair)
+        key = jnp.where(live, row_tile, row_tiles)
+        ordered, perm, keep, end, held = sort_tables(key)
+        table(3, perm)
+        table(4, jnp.where(held > 0, end, 2 * slots))
+        table(5, ordered(week))
+        lane = lax.broadcasted_iota(jnp.int32, (1, TILE), 1)
+        table(6, ordered(cell_block + jnp.where(lane < slots, 0, per_dev)))
+        table(7, jnp.zeros((1, TILE), jnp.int32))
+        share_tab[1:2, :] = keep.astype(jnp.float32)
+        share_tab[2:8, :] = jnp.zeros((6, TILE), jnp.float32)
+        for i, (src, dst) in enumerate(((whole_tab, whole_s), (share_tab, share_s))):
+            copy = pltpu.make_async_copy(src, dst, tab_sem.at[i])
+            copy.start()
+            copy.wait()
+
+    def on_block(q, ch):
+        @pl.loop(0, part)
+        def _(s):
+            t = q * slots + ch * part + s
+            products[t] = lax.dot_general(
+                covar[q * per_dev + whole_s[2, t]], tiles[t], (((1,), (1,)), ((), ())),
+                preferred_element_type=jnp.float32,
+            )
+
+    gather_phase(
+        chips, lines, own, packet, info, tiles, home_tiles, covar,
+        packets, infos, home_pos, pkt_send, pkt_recv, sib_send, sib_recv, hop_send, hop_recv,
+        on_places, on_block,
+    )
+
+    decay = jnp.exp(jnp.float32(-1.0 / TIME_RANGE))
+    step_rows = runs.shape[1]
+    runs[total] = jnp.zeros((step_rows, TILE), jnp.float32)
+
+    steps = TILE // step_rows
+
+    @pl.loop(0, homes // step_rows)
+    def _(i):
+        strip = pl.ds(pl.multiple_of(i * step_rows, step_rows), step_rows)
+        inner = pl.ds(pl.multiple_of((i % steps) * step_rows, step_rows), step_rows)
+        running = jnp.zeros((step_rows, TILE), jnp.float32)
+        for n in range(total):
+            running = running * share_s[0, n] + products[whole_s[0, n], strip, :]
+            runs[n] = running
+        for r in range(row_tiles):
+            spread = [runs[whole_s[1, r * WEEKS + w]] for w in range(WEEKS)]
+            ahead = [spread[0]]
+            for w in range(1, WEEKS):
+                ahead.append(spread[w] + decay * ahead[-1])
+            back = None
+            for w in reversed(range(WEEKS)):
+                value = ahead[w] if back is None else ahead[w] + back
+                weighted[w, i // steps, inner, r * TILE : (r + 1) * TILE] = value.astype(jnp.bfloat16)
+                back = decay * (spread[w] if back is None else spread[w] + back)
+
+    home_runs[2 * slots] = jnp.zeros((TILE, OBS), jnp.float32)
+
+    @pl.loop(0, 2 * slots)
+    def _(n):
+        value = jnp.dot(
+            home_tiles[whole_s[3, n]], weighted[whole_s[5, n], whole_s[6, n]],
+            preferred_element_type=jnp.float32,
+        )
+        before = home_runs[lax.rem(n + 2 * slots, 2 * slots + 1)]
+        home_runs[n] = value + before * share_s[1, n]
+
+    def half(q, k):
+        return home_runs[whole_s[4, q], pl.ds(pl.multiple_of(k * rows, 8), rows), :]
+
+    for q in range(chips):
+        sib_out[q] = half(q, 1 - core)
+
+    reduce_phase(
+        chips, lines, obs, out, sib, y_out, y_in, z_out, z_in,
+        ex_send, ex_recv, y_send, y_recv, z_send, z_recv,
+        lambda q: sib_out.at[q], lambda q: half(q, core),
+    )
 
 
 def local(footprints, tile_rows, tile_cols, tile_counts, coords, obs_error):
@@ -353,36 +573,83 @@
     smem = pl.BlockSpec(memory_space=pltpu.SMEM)
     dma = pltpu.SemaphoreType.DMA
 
-    places = jnp.concatenate([tile_rows, tile_cols, tile_counts]).astype(jnp.float32)
-    places = jnp.pad(places, (0, TILE - places.shape[0]))
-    packet = jnp.concatenate([coords.reshape(2 * per_dev, TILE), places[None, :]], axis=0)
+    info = jnp.concatenate([tile_rows, tile_cols, tile_counts])
+    info = jnp.pad(info[None, :], ((0, 7), (0, TILE - info.shape[0])))
+    packet = coords.reshape(2 * per_dev, TILE)
     packet = jnp.pad(packet, ((0, 8 - packet.shape[0]), (0, 0)))
+
+    f32, bf16 = jnp.float32, jnp.bfloat16
+    gather_scratch = [
+        pltpu.VMEM((chips + 1, 8, TILE), f32),
+        pltpu.VMEM((chips + 1, 8, TILE), jnp.int32),
+        pltpu.VMEM((2, 2 * cells, TILE), f32),
+        dma((2, chips)),
+        dma((2, chips)),
+        dma,
+        dma,
+        dma((4, depth, CHUNKS)),
+        dma((chips * CHUNKS,)),
+    ]
+    reduce_scratch = [
+        pltpu.VMEM((chips, rows, OBS), f32),
+        pltpu.VMEM((depth, rows, OBS), bf16),
+        pltpu.VMEM((depth, rows, OBS), bf16),
+        pltpu.VMEM((depth, rows, OBS), bf16),
+        pltpu.VMEM((2, depth, rows, OBS), bf16),
+        dma((chips,)),
+        dma((chips,)),
+        dma((depth,)),
+        dma((depth,)),
+        dma((depth,)),
+        dma((2, depth)),
+    ]
+    if chips * slots < TILE and chips * TILE == OBS:
+        total = chips * slots
+        return pl.pallas_call(
+            functools.partial(fused_kernel, chips, lines),
+            out_shape=jax.ShapeDtypeStruct((rows, OBS), f32),
+            in_specs=[vmem] * 4,
+            out_specs=vmem,
+            scratch_shapes=[
+                pltpu.VMEM((total, TILE, TILE), bf16),
+                pltpu.VMEM((2 * slots, TILE, TILE), bf16),
+                pltpu.VMEM((chips * per_dev, 2 * cells, TILE), bf16),
+                pltpu.VMEM((total, 2 * cells, TILE), f32),
+                pltpu.VMEM((total + 1, 32, TILE), f32),
+                pltpu.VMEM((WEEKS, 2 * per_dev, TILE, OBS), bf16),
+                pltpu.VMEM((2 * slots + 1, TILE, OBS), f32),
+                pltpu.VMEM((chips, rows, OBS), f32),
+                pltpu.VMEM((TILE, TILE), jnp.int32),
+                pltpu.VMEM((8, TILE), jnp.int32),
+                pltpu.VMEM((8, TILE), f32),
+                pltpu.SMEM((8, TILE), jnp.int32),
+                pltpu.SMEM((8, TILE), f32),
+                dma((2,)),
+                *gather_scratch,
+                *reduce_scratch,
+            ],
+            compiler_params=pltpu.CompilerParams(
+                collective_id=0, has_side_effects=True, vmem_limit_bytes=VMEM_BYTES
+            ),
+            name="fused",
+        )(footprints, packet, info, obs_error.reshape(1, rows))
 
     tiles, home_tiles, covar, meta = pl.pallas_call(
         functools.partial(gather_kernel, chips, lines),
         out_shape=(
-            jax.ShapeDtypeStruct((chips * slots, TILE, TILE), jnp.bfloat16),
-            jax.ShapeDtypeStruct((2 * slots, TILE, TILE), jnp.bfloat16),
-            jax.ShapeDtypeStruct((chips * per_dev, 2 * cells, TILE), jnp.bfloat16),
+            jax.ShapeDtypeStruct((chips * slots, TILE, TILE), bf16),
+            jax.ShapeDtypeStruct((2 * slots, TILE, TILE), bf16),
+            jax.ShapeDtypeStruct((chips * per_dev, 2 * cells, TILE), bf16),
             jax.ShapeDtypeStruct((chips + 2, 8, TILE), jnp.int32),
         ),
-        in_specs=[vmem] * 2,
+        in_specs=[vmem] * 3,
         out_specs=(vmem,) * 4,
-        scratch_shapes=[
-            pltpu.VMEM((chips + 1, 8, TILE), jnp.float32),
-            pltpu.VMEM((2, 2 * cells, TILE), jnp.float32),
-            dma((chips,)),
-            dma((chips,)),
-            dma,
-            dma,
-            dma((4, depth, CHUNKS)),
-            dma((chips * CHUNKS,)),
-        ],
+        scratch_shapes=gather_scratch,
         compiler_params=pltpu.CompilerParams(
             collective_id=0, has_side_effects=True, vmem_limit_bytes=VMEM_BYTES
         ),
         name="gather",
-    )(footprints, packet)
+    )(footprints, packet, info)
 
     partial = pl.pallas_call(
         functools.partial(spread_kernel, chips),
@@ -399,22 +666,10 @@
 
     return pl.pallas_call(
         functools.partial(reduce_kernel, chips, lines),
-        out_shape=jax.ShapeDtypeStruct((rows, OBS), jnp.float32),
+        out_shape=jax.ShapeDtypeStruct((rows, OBS), f32),
         in_specs=[vmem] * 2,
         out_specs=vmem,
-        scratch_shapes=[
-            pltpu.VMEM((chips, rows, OBS), jnp.float32),
-            pltpu.VMEM((depth, rows, OBS), jnp.bfloat16),
-            pltpu.VMEM((depth, rows, OBS), jnp.bfloat16),
-            pltpu.VMEM((depth, rows, OBS), jnp.bfloat16),
-            pltpu.VMEM((2, depth, rows, OBS), jnp.bfloat16),
-            dma((chips,)),
-            dma((chips,)),
-            dma((depth,)),
-            dma((depth,)),
-            dma((depth,)),
-            dma((2, depth)),
-        ],
+        scratch_shapes=reduce_scratch,
         compiler_params=pltpu.CompilerParams(
             collective_id=1, has_side_effects=True, vmem_limit_bytes=VMEM_BYTES
         ),

time: 84.3 us -> 70.9 us (0.84)
  Pallas kernels: 80 us -> 66.4 us
  other arithmetic: 1.35 us -> 0.08 us
  local copies, waits for them, and re-layouts: 2.37 us -> 3.46 us
    pallas_call x3 -> x1, Pallas kernels: 80 us -> 66.4 us  [local(): pl.pallas_call(functools.partial(fused_kernel, chips, lines), out_shape=j...]
    pad x0 -> x2, local copies, waits for them, and re-layouts: none -> 1.19 us  [the longest x1 0.6 us: local(): packet = jnp.pad(packet, ((0, 8 - packet.shape[0]), (0, 0)))]
    unnamed x1 -> x7, local copies, waits for them, and re-layouts: 1.67 us -> 2.26 us
where the time goes in v2:
time: 70.9 us; the launch traced here: 70.7 us
  Pallas kernels  66.4 us (94%)
  local copies, waits for them, and re-layouts  3.46 us (5%)
  between operations  0.72 us (1%)
    pallas_call x1, Pallas kernels, local(): pl.pallas_call(functools.partial(fused_kernel, chips, lines), out_shape=j...  66.4 us
    unnamed x7, local copies, waits for them, and re-layouts  2.26 us

profile of v2, /device:TPU:0, one launch (start us, length us, event | category | flops | bytes accessed | tf_op | source)
XLA Modules:
  0.0 70.7 jit_solution(14839203653447317780)
XLA Ops:
  0.0 0.0 copy-start.1
  0.0 0.0 copy-start.2
  0.7 0.0 copy-start
  0.7 0.0 copy-done.1
  0.7 0.0 copy-done.2
  0.7 0.1 add_bitcast_fusion
  0.8 0.6 copy-done
  1.4 0.6 pad.8.packet
  2.0 0.6 pad.9.info
  2.6 66.4 %fused.1 = f32[64,1024]{1,0:T(8,128)} custom-call(bf16[8,128,128]{2,1,0:T(8,128)(2,1)} %own.1, f32[8,128]{1,0:T(8,128)} %pad.8.packet, s32[8,128]{1,0:T(8,128)} %pad.9.info, f32[1,64]{1,0:T(1,128)} %bitcast.3), custom_call_target="tpu_custom_call" | custom-call | tf_op jit(solution)/shard_map/fused/pallas_call | solution.py:608
  69.0 1.7 %copy.9 = f32[64,1024]{1,0:T(8,128)} copy(f32[64,1024]{1,0:T(8,128)} %fused.1) | data formatting | bytes 524288
  (1 shorter events, 0.0 us)
Async XLA Ops:
  0.0 0.7 copy-start.1
  0.0 0.7 copy-start.2
  0.7 0.7 copy-start

commit v3 on v2

--- a/solution.py
+++ b/solution.py
@@ -13,6 +13,7 @@
 SPACE_RANGE = 1.0
 TIME_RANGE = 3.0
 CHUNKS = 2
+SPLIT = 2
 VMEM_BYTES = 56 * 1024 * 1024
 
 
@@ -40,8 +41,8 @@
 
 
 def gather_phase(
-    chips, lines, own, packet, info, tiles, home_tiles, covar,
-    packets, infos, home_pos, pkt_send, pkt_recv, sib_send, sib_recv, hop_send, hop_recv,
+    chips, lines, own, coords, raw, tiles, home_tiles, covar,
+    packet, info, packets, infos, home_pos, pkt_send, pkt_recv, sib_send, sib_recv, hop_send, hop_recv,
     on_places, on_block=None,
 ):
     depth = chips // lines
@@ -57,6 +58,16 @@
         signal(barrier, lax.rem(chip + k, chips) * 2 + core)
     signal(barrier, sibling)
     pl.semaphore_wait(barrier, chips)
+
+    packet[...] = jnp.zeros_like(packet)
+    for axis in range(2):
+        for b in range(per_dev):
+            packet[axis * per_dev + b : axis * per_dev + b + 1, :] = coords[
+                axis : axis + 1, b * TILE : (b + 1) * TILE
+            ]
+    info[...] = jnp.zeros_like(info)
+    for i, ref in enumerate(raw):
+        info[i : i + 1, 0 : ref.shape[1]] = ref[...]
 
     pkt_copies = []
     for i, (src, dst) in enumerate(((packet, packets), (info, infos))):
@@ -200,8 +211,8 @@
 
 
 def gather_kernel(
-    chips, lines, own, packet, info, tiles, home_tiles, covar, meta,
-    packets, infos, home_pos, pkt_send, pkt_recv, sib_send, sib_recv, hop_send, hop_recv,
+    chips, lines, own, coords, row_in, col_in, count_in, tiles, home_tiles, covar, meta,
+    packet, info, packets, infos, home_pos, pkt_send, pkt_recv, sib_send, sib_recv, hop_send, hop_recv,
 ):
     def on_places(pair):
         for q in range(chips):
@@ -210,8 +221,8 @@
             meta[chips + j] = pair[j]
 
     gather_phase(
-        chips, lines, own, packet, info, tiles, home_tiles, covar,
-        packets, infos, home_pos, pkt_send, pkt_recv, sib_send, sib_recv, hop_send, hop_recv,
+        chips, lines, own, coords, (row_in, col_in, count_in), tiles, home_tiles, covar,
+        packet, info, packets, infos, home_pos, pkt_send, pkt_recv, sib_send, sib_recv, hop_send, hop_recv,
         on_places,
     )
 
@@ -228,12 +239,12 @@
         acc[i] = jnp.zeros((homes, TILE), jnp.float32)
 
     def place_of(d, s):
-        col = meta[d, 0, slots + s]
+        col = meta[d, 1, s]
         return meta[d, 0, s], col // per_dev, col % per_dev
 
     @pl.loop(0, chips)
     def _(q):
-        @pl.loop(0, meta[q, 0, 2 * slots])
+        @pl.loop(0, meta[q, 2, 0])
         def _(s):
             row, week, b = place_of(q, s)
             strip = covar[q * per_dev + b]
@@ -261,7 +272,7 @@
 
     out[...] = jnp.zeros_like(out)
     for j in range(2):
-        @pl.loop(0, meta[chips + j, 0, 2 * slots])
+        @pl.loop(0, meta[chips + j, 2, 0])
         def _(s):
             row, week, b = place_of(chips + j, s)
             slab = weighted[week, pl.ds(pl.multiple_of(j * cells + b * TILE, TILE), TILE), :]
@@ -273,18 +284,18 @@
 
 def reduce_phase(
     chips, lines, obs, out, sib, y_out, y_in, z_out, z_in,
-    sib_send, sib_recv, y_send, y_recv, z_send, z_recv, outgoing, mine,
+    sib_send, sib_recv, y_send, y_recv, z_send, z_recv, prepare, outgoing, mine,
 ):
     depth = chips // lines
     me, core, chip, y, z = place(lines)
     sibling = me + 1 - 2 * core
     rows = out.shape[0]
+    width = out.shape[1] // SPLIT
     above = me + 2 * lines
     below = me - 2 * lines
     across = me + 2 - 4 * y
     up_ok = z < depth - 1
     down_ok = z > 0
-
     upper = (z >= depth // 2).astype(jnp.int32)
 
     def order(j):
@@ -295,88 +306,103 @@
         low = j + (j >= z).astype(jnp.int32)
         return upper * low + (1 - upper) * high
 
-    def sib_copy(q):
-        return remote(outgoing(q), sib.at[q], sib_send.at[q], sib_recv.at[q], sibling)
-
-    columns = list(reversed(range(lines)))
-    for line in columns:
-        for j in range(depth):
-            sib_copy(order(j) * lines + (y + line) % lines).start()
-
-    def chip_sum(q):
-        sib_copy(q).wait_recv()
-        return mine(q) + sib[q]
-
-    if lines == 2:
+    def sib_copy(h, q):
+        return remote(
+            outgoing(h, q), sib.at[h, q], sib_send.at[h, q], sib_recv.at[h, q], sibling
+        )
+
+    def chip_sum(h, q):
+        sib_copy(h, q).wait_recv()
+        return mine(h, q) + sib[h, q]
+
+    def y_copy(h, c):
+        return remote(y_out.at[h, c], y_in.at[h, c], y_send.at[h, c], y_recv.at[h, c], across)
+
+    def up_copy(h, c):
+        return remote(z_out.at[h, c], z_in.at[h, 0, c], z_send.at[h, c], z_recv.at[h, 0, c], above)
+
+    def down_copy(h, c):
+        return remote(z_out.at[h, c], z_in.at[h, 1, c], z_send.at[h, c], z_recv.at[h, 1, c], below)
+
+    def y_stage(h):
         for j in range(depth):
             c = order(j)
-            y_out[c] = chip_sum(c * lines + 1 - y).astype(jnp.bfloat16)
-            remote(y_out.at[c], y_in.at[c], y_send.at[c], y_recv.at[c], across).start()
-
-    def up_copy(c):
-        return remote(z_out.at[c], z_in.at[0, c], z_send.at[c], z_recv.at[0, c], above)
-
-    def down_copy(c):
-        return remote(z_out.at[c], z_in.at[1, c], z_send.at[c], z_recv.at[1, c], below)
+            y_out[h, c] = chip_sum(h, c * lines + 1 - y).astype(jnp.bfloat16)
+            y_copy(h, c).start()
+
+    for h in range(SPLIT):
+        prepare(h)
+        for line in reversed(range(lines)):
+            for j in range(depth):
+                sib_copy(h, order(j) * lines + (y + line) % lines).start()
+        if lines == 2 and h > 0:
+            y_stage(h - 1)
+    if lines == 2:
+        y_stage(SPLIT - 1)
+
+    def column_sum(h, c):
+        total = chip_sum(h, c * lines + y)
+        if lines == 2:
+            y_copy(h, c).wait_recv()
+            total = total + y_in[h, c].astype(jnp.float32)
+        return total
 
     for j in range(depth - 1):
-        c = order(j)
-        total = chip_sum(c * lines + y)
-        if lines == 2:
-            remote(y_out.at[c], y_in.at[c], y_send.at[c], y_recv.at[c], across).wait_recv()
-            total = total + y_in[c].astype(jnp.float32)
-        out[...] = total
-
-        @pl.when((c > z) & down_ok)
-        def _():
-            up_copy(c).wait_recv()
-            out[...] += z_in[0, c].astype(jnp.float32)
-
-        @pl.when((c < z) & up_ok)
-        def _():
-            down_copy(c).wait_recv()
-            out[...] += z_in[1, c].astype(jnp.float32)
-
-        z_out[c] = out[...].astype(jnp.bfloat16)
-
-        @pl.when(c > z)
-        def _():
-            up_copy(c).start()
-
-        @pl.when(c < z)
-        def _():
-            down_copy(c).start()
-
-    total = chip_sum(chip)
-    if lines == 2:
-        remote(y_out.at[z], y_in.at[z], y_send.at[z], y_recv.at[z], across).wait_recv()
-        total = total + y_in[z].astype(jnp.float32)
+        for h in range(SPLIT):
+            c = order(j)
+            part = (slice(None), slice(h * width, (h + 1) * width))
+            out[part] = column_sum(h, c)
+
+            @pl.when((c > z) & down_ok)
+            def _():
+                up_copy(h, c).wait_recv()
+                out[part] += z_in[h, 0, c].astype(jnp.float32)
+
+            @pl.when((c < z) & up_ok)
+            def _():
+                down_copy(h, c).wait_recv()
+                out[part] += z_in[h, 1, c].astype(jnp.float32)
+
+            z_out[h, c] = out[part].astype(jnp.bfloat16)
+
+            @pl.when(c > z)
+            def _():
+                up_copy(h, c).start()
+
+            @pl.when(c < z)
+            def _():
+                down_copy(h, c).start()
+
     shape = (rows, rows)
     eye = lax.broadcasted_iota(jnp.int32, shape, 0) == lax.broadcasted_iota(jnp.int32, shape, 1)
     errors = jnp.sum(
         jnp.where(eye, jnp.broadcast_to(obs[...], shape), 0.0), axis=1, keepdims=True
     )
-    hit = lax.broadcasted_iota(jnp.int32, out.shape, 1) == (
-        me * rows + lax.broadcasted_iota(jnp.int32, out.shape, 0)
-    )
-    out[...] = total + jnp.where(hit, jnp.broadcast_to(errors, out.shape), 0.0)
-
-    @pl.when(down_ok)
-    def _():
-        up_copy(z).wait_recv()
-        out[...] += z_in[0, z].astype(jnp.float32)
-
-    @pl.when(up_ok)
-    def _():
-        down_copy(z).wait_recv()
-        out[...] += z_in[1, z].astype(jnp.float32)
-
-    for q in range(chips):
-        sib_copy(q).wait_send()
-    for c in range(depth):
-        if lines == 2:
-            remote(y_out.at[c], y_in.at[c], y_send.at[c], y_recv.at[c], across).wait_send()
-        pl.when(c != z)(lambda c=c: up_copy(c).wait_send())
+    for h in range(SPLIT):
+        part = (slice(None), slice(h * width, (h + 1) * width))
+        block = (rows, width)
+        hit = h * width + lax.broadcasted_iota(jnp.int32, block, 1) == (
+            me * rows + lax.broadcasted_iota(jnp.int32, block, 0)
+        )
+        out[part] = column_sum(h, z) + jnp.where(hit, jnp.broadcast_to(errors, block), 0.0)
+
+        @pl.when(down_ok)
+        def _():
+            up_copy(h, z).wait_recv()
+            out[part] += z_in[h, 0, z].astype(jnp.float32)
+
+        @pl.when(up_ok)
+        def _():
+            down_copy(h, z).wait_recv()
+            out[part] += z_in[h, 1, z].astype(jnp.float32)
+
+    for h in range(SPLIT):
+        for q in range(chips):
+            sib_copy(h, q).wait_send()
+        for c in range(depth):
+            if lines == 2:
+                y_copy(h, c).wait_send()
+            pl.when(c != z)(lambda: up_copy(h, c).wait_send())
 
 
 def reduce_kernel(chips, lines, partial, obs, out, *scratch):
@@ -398,12 +424,16 @@
     pl.when(down_ok)(lambda: signal(barrier, below))
     pl.semaphore_wait(barrier, lines + up_ok.astype(jnp.int32) + down_ok.astype(jnp.int32))
 
-    def slab(q, k):
-        return partial.at[pl.ds(pl.multiple_of((q * 2 + k) * rows, 8), rows)]
+    width = out.shape[1] // SPLIT
+
+    def slab(h, q, k):
+        return partial.at[
+            pl.ds(pl.multiple_of((q * 2 + k) * rows, 8), rows), pl.ds(h * width, width)
+        ]
 
     reduce_phase(
         chips, lines, obs, out, *scratch,
-        lambda q: slab(q, 1 - core), lambda q: slab(q, core)[...],
+        lambda h: None, lambda h, q: slab(h, q, 1 - core), lambda h, q: slab(h, q, core)[...],
     )
 
 
@@ -433,10 +463,10 @@
 
 
 def fused_kernel(
-    chips, lines, own, packet, info, obs, out,
+    chips, lines, own, coords, row_in, col_in, count_in, obs, out,
     tiles, home_tiles, covar, products, runs, weighted, home_runs, sib_out,
     places, whole_tab, share_tab, whole_s, share_s, tab_sem,
-    packets, infos, home_pos, pkt_send, pkt_recv, sib_send, sib_recv, hop_send, hop_recv,
+    packet, info, packets, infos, home_pos, pkt_send, pkt_recv, sib_send, sib_recv, hop_send, hop_recv,
     sib, y_out, y_in, z_out, z_in, ex_send, ex_recv, y_send, y_recv, z_send, z_recv,
 ):
     slots = own.shape[0]
@@ -451,20 +481,19 @@
 
     def places_of(values):
         n = len(values) * slots
-        places[...] = jnp.zeros((TILE, TILE), jnp.int32)
-        for i, value in enumerate(values):
-            places[i * slots : (i + 1) * slots, :] = jnp.broadcast_to(
-                value[0:1, :], (slots, TILE)
-            )
-        known = jnp.transpose(places[...])
         row = lax.broadcasted_iota(jnp.int32, (TILE, TILE), 0)
         lane = lax.broadcasted_iota(jnp.int32, (TILE, TILE), 1)
         slot = lane % slots
-
-        def pick(at):
-            return jnp.sum(jnp.where(row == at, known, 0), axis=0, keepdims=True)
-
-        row_tile, col_tile, count = pick(slot), pick(slots + slot), pick(2 * slots)
+        picked = []
+        for k, at in enumerate((slot, slot, 0)):
+            places[k] = jnp.zeros((TILE, TILE), jnp.int32)
+            for i, value in enumerate(values):
+                places[k, i * slots : (i + 1) * slots, :] = jnp.broadcast_to(
+                    value[k : k + 1, :], (slots, TILE)
+                )
+            known = jnp.transpose(places[k])
+            picked.append(jnp.sum(jnp.where(row == at, known, 0), axis=0, keepdims=True))
+        row_tile, col_tile, count = picked
         live = (slot[0:1, :] < count) & (lane[0:1, :] < n)
         week = lax.shift_right_logical(col_tile, jnp.full_like(col_tile, per_dev // 2))
         return row_tile, week, col_tile - per_dev * week, live
@@ -506,8 +535,8 @@
             )
 
     gather_phase(
-        chips, lines, own, packet, info, tiles, home_tiles, covar,
-        packets, infos, home_pos, pkt_send, pkt_recv, sib_send, sib_recv, hop_send, hop_recv,
+        chips, lines, own, coords, (row_in, col_in, count_in), tiles, home_tiles, covar,
+        packet, info, packets, infos, home_pos, pkt_send, pkt_recv, sib_send, sib_recv, hop_send, hop_recv,
         on_places, on_block,
     )
 
@@ -536,27 +565,31 @@
                 weighted[w, i // steps, inner, r * TILE : (r + 1) * TILE] = value.astype(jnp.bfloat16)
                 back = decay * (spread[w] if back is None else spread[w] + back)
 
-    home_runs[2 * slots] = jnp.zeros((TILE, OBS), jnp.float32)
-
-    @pl.loop(0, 2 * slots)
-    def _(n):
-        value = jnp.dot(
-            home_tiles[whole_s[3, n]], weighted[whole_s[5, n], whole_s[6, n]],
-            preferred_element_type=jnp.float32,
-        )
-        before = home_runs[lax.rem(n + 2 * slots, 2 * slots + 1)]
-        home_runs[n] = value + before * share_s[1, n]
-
-    def half(q, k):
-        return home_runs[whole_s[4, q], pl.ds(pl.multiple_of(k * rows, 8), rows), :]
-
-    for q in range(chips):
-        sib_out[q] = half(q, 1 - core)
+    width = OBS // SPLIT
+
+    def half(h, q, k):
+        return home_runs[h, whole_s[4, q], pl.ds(pl.multiple_of(k * rows, 8), rows), :]
+
+    def prepare(h):
+        home_runs[h, 2 * slots] = jnp.zeros((TILE, width), jnp.float32)
+
+        @pl.loop(0, 2 * slots, unroll=4)
+        def _(n):
+            value = jnp.dot(
+                home_tiles[whole_s[3, n]],
+                weighted[whole_s[5, n], whole_s[6, n], :, pl.ds(h * width, width)],
+                preferred_element_type=jnp.float32,
+            )
+            before = home_runs[h, lax.rem(n + 2 * slots, 2 * slots + 1)]
+            home_runs[h, n] = value + before * share_s[1, n]
+
+        for q in range(chips):
+            sib_out[h, q] = half(h, q, 1 - core)
 
     reduce_phase(
         chips, lines, obs, out, sib, y_out, y_in, z_out, z_in,
         ex_send, ex_recv, y_send, y_recv, z_send, z_recv,
-        lambda q: sib_out.at[q], lambda q: half(q, core),
+        prepare, lambda h, q: sib_out.at[h, q], lambda h, q: half(h, q, core),
     )
 
 
@@ -573,13 +606,13 @@
     smem = pl.BlockSpec(memory_space=pltpu.SMEM)
     dma = pltpu.SemaphoreType.DMA
 
-    info = jnp.concatenate([tile_rows, tile_cols, tile_counts])
-    info = jnp.pad(info[None, :], ((0, 7), (0, TILE - info.shape[0])))
-    packet = coords.reshape(2 * per_dev, TILE)
-    packet = jnp.pad(packet, ((0, 8 - packet.shape[0]), (0, 0)))
-
+    places = (
+        tile_rows.reshape(1, slots), tile_cols.reshape(1, slots), tile_counts.reshape(1, 1)
+    )
     f32, bf16 = jnp.float32, jnp.bfloat16
     gather_scratch = [
+        pltpu.VMEM((8, TILE), f32),
+        pltpu.VMEM((8, TILE), jnp.int32),
         pltpu.VMEM((chips + 1, 8, TILE), f32),
         pltpu.VMEM((chips + 1, 8, TILE), jnp.int32),
         pltpu.VMEM((2, 2 * cells, TILE), f32),
@@ -590,25 +623,26 @@
         dma((4, depth, CHUNKS)),
         dma((chips * CHUNKS,)),
     ]
+    width = OBS // SPLIT
     reduce_scratch = [
-        pltpu.VMEM((chips, rows, OBS), f32),
-        pltpu.VMEM((depth, rows, OBS), bf16),
-        pltpu.VMEM((depth, rows, OBS), bf16),
-        pltpu.VMEM((depth, rows, OBS), bf16),
-        pltpu.VMEM((2, depth, rows, OBS), bf16),
-        dma((chips,)),
-        dma((chips,)),
-        dma((depth,)),
-        dma((depth,)),
-        dma((depth,)),
-        dma((2, depth)),
+        pltpu.VMEM((SPLIT, chips, rows, width), f32),
+        pltpu.VMEM((SPLIT, depth, rows, width), bf16),
+        pltpu.VMEM((SPLIT, depth, rows, width), bf16),
+        pltpu.VMEM((SPLIT, depth, rows, width), bf16),
+        pltpu.VMEM((SPLIT, 2, depth, rows, width), bf16),
+        dma((SPLIT, chips)),
+        dma((SPLIT, chips)),
+        dma((SPLIT, depth)),
+        dma((SPLIT, depth)),
+        dma((SPLIT, depth)),
+        dma((SPLIT, 2, depth)),
     ]
     if chips * slots < TILE and chips * TILE == OBS:
         total = chips * slots
         return pl.pallas_call(
             functools.partial(fused_kernel, chips, lines),
             out_shape=jax.ShapeDtypeStruct((rows, OBS), f32),
-            in_specs=[vmem] * 4,
+            in_specs=[vmem] * 6,
             out_specs=vmem,
             scratch_shapes=[
                 pltpu.VMEM((total, TILE, TILE), bf16),
@@ -617,9 +651,9 @@
                 pltpu.VMEM((total, 2 * cells, TILE), f32),
                 pltpu.VMEM((total + 1, 32, TILE), f32),
                 pltpu.VMEM((WEEKS, 2 * per_dev, TILE, OBS), bf16),
-                pltpu.VMEM((2 * slots + 1, TILE, OBS), f32),
-                pltpu.VMEM((chips, rows, OBS), f32),
-                pltpu.VMEM((TILE, TILE), jnp.int32),
+                pltpu.VMEM((SPLIT, 2 * slots + 1, TILE, width), f32),
+                pltpu.VMEM((SPLIT, chips, rows, width), f32),
+                pltpu.VMEM((3, TILE, TILE), jnp.int32),
                 pltpu.VMEM((8, TILE), jnp.int32),
                 pltpu.VMEM((8, TILE), f32),
                 pltpu.SMEM((8, TILE), jnp.int32),
@@ -632,7 +666,7 @@
                 collective_id=0, has_side_effects=True, vmem_limit_bytes=VMEM_BYTES
             ),
             name="fused",
-        )(footprints, packet, info, obs_error.reshape(1, rows))
+        )(footprints, coords, *places, obs_error.reshape(1, rows))
 
     tiles, home_tiles, covar, meta = pl.pallas_call(
         functools.partial(gather_kernel, chips, lines),
@@ -642,14 +676,14 @@
             jax.ShapeDtypeStruct((chips * per_dev, 2 * cells, TILE), bf16),
             jax.ShapeDtypeStruct((chips + 2, 8, TILE), jnp.int32),
         ),
-        in_specs=[vmem] * 3,
+        in_specs=[vmem] * 5,
         out_specs=(vmem,) * 4,
         scratch_shapes=gather_scratch,
         compiler_params=pltpu.CompilerParams(
             collective_id=0, has_side_effects=True, vmem_limit_bytes=VMEM_BYTES
         ),
         name="gather",
-    )(footprints, packet, info)
+    )(footprints, coords, *places)
 
     partial = pl.pallas_call(
         functools.partial(spread_kernel, chips),

time: 70.9 us -> 69.3 us (0.977)
  local copies, waits for them, and re-layouts: 3.46 us -> 1.67 us
    pad x2 -> x0, local copies, waits for them, and re-layouts: 1.19 us -> none  [the longest x1 0.6 us: local(): packet = jnp.pad(packet, ((0, 8 - packet.shape[0]), (0, 0)))]
    unnamed x7 -> x1, local copies, waits for them, and re-layouts: 2.26 us -> 1.67 us
where the time goes in v3:
time: 69.3 us; the launch traced here: 69.2 us
  Pallas kernels  66.8 us (96%)
  local copies, waits for them, and re-layouts  1.67 us (2%)
    pallas_call x1, Pallas kernels, local(): pl.pallas_call(functools.partial(fused_kernel, chips, lines), out_shape=j...  66.8 us
    unnamed x1, local copies, waits for them, and re-layouts  1.67 us

profile of v3, /device:TPU:0, one launch (start us, length us, event | category | flops | bytes accessed | tf_op | source)
XLA Modules:
  0.0 69.2 jit_solution(15350219889691163647)
XLA Ops:
  0.7 66.8 %fused.1 = f32[64,1024]{1,0:T(8,128)} custom-call(bf16[8,128,128]{2,1,0:T(8,128)(2,1)} %own.1, f32[2,256]{1,0:T(2,128)} %coords.1, s32[1,8]{1,0:T(1,128)} %bitcast.5, s32[1,8]{1,0:T(1,128)} %bitcast.6, s32[1,1]{1,0:T(1,128)} %bitcast.4.count_in, f32[1,64]{1,0:T(1,128)} %bitcast.7), custom_call_target="tpu_custom_call" | custom-call | tf_op jit(solution)/shard_map/fused/pallas_call | solution.py:642
  67.5 1.7 %copy.9 = f32[64,1024]{1,0:T(8,128)} copy(f32[64,1024]{1,0:T(8,128)} %fused.1) | data formatting | bytes 524288

commit v4 on v3

--- a/solution.py
+++ b/solution.py
@@ -123,10 +123,6 @@
     other = packets[chips]
     is_first = (core == 0).astype(jnp.float32)
     pair = (mine * is_first + other * (1.0 - is_first), other * is_first + mine * (1.0 - is_first))
-    first = jnp.broadcast_to(core == 0, info.shape)
-    on_places((
-        jnp.where(first, info[...], infos[chips]), jnp.where(first, infos[chips], info[...])
-    ))
     for j in range(2):
         columns = jnp.transpose(pair[j])
         for b in range(per_dev):
@@ -137,8 +133,7 @@
 
     step_rows = 64
 
-    @pl.loop(0, chips)
-    def _(q):
+    def distances(q):
         for b in range(per_dev):
             east = packets[q, b : b + 1, :]
             north = packets[q, per_dev + b : per_dev + b + 1, :]
@@ -169,8 +164,7 @@
         if d > 0:
             pl.when(z + d < depth)(high)
 
-    for ch in range(CHUNKS):
-        done(chip, ch)
+    pl.loop(0, chips // 2)(distances)
 
     for d in range(1, depth):
         for ch in range(CHUNKS):
@@ -192,6 +186,15 @@
                 send((z + d < depth) & (z > 0), 1, d, q_high, ch, below, False)
             if lines == 2:
                 send(z + d < depth, 3, d, q_high, ch, across, False)
+            if d == 1 and ch == 0:
+                pl.loop(chips // 2, chips)(distances)
+        if d == 1:
+            first = jnp.broadcast_to(core == 0, info.shape)
+            on_places((
+                jnp.where(first, info[...], infos[chips]), jnp.where(first, infos[chips], info[...])
+            ))
+            for ch in range(CHUNKS):
+                done(chip, ch)
         for ch in range(CHUNKS):
             if on_block is not None:
                 pl.when(z >= d)(lambda: on_block((z - d) * lines + y, ch))
@@ -347,8 +350,8 @@
             total = total + y_in[h, c].astype(jnp.float32)
         return total
 
-    for j in range(depth - 1):
-        for h in range(SPLIT):
+    for h in range(SPLIT):
+        for j in range(depth - 1):
             c = order(j)
             part = (slice(None), slice(h * width, (h + 1) * width))
             out[part] = column_sum(h, c)

time: 69.3 us -> 66.5 us (0.960)
  Pallas kernels: 66.8 us -> 64 us
    pallas_call x1, Pallas kernels: 66.8 us -> 64 us  [local(): pl.pallas_call(functools.partial(fused_kernel, chips, lines), out_shape=j...]
where the time goes in v4:
time: 66.5 us; the launch traced here: 66.3 us
  Pallas kernels  64 us (96%)
  local copies, waits for them, and re-layouts  1.67 us (3%)
    pallas_call x1, Pallas kernels, local(): pl.pallas_call(functools.partial(fused_kernel, chips, lines), out_shape=j...  64 us
    unnamed x1, local copies, waits for them, and re-layouts  1.67 us

profile of v4, /device:TPU:0, one launch (start us, length us, event | category | flops | bytes accessed | tf_op | source)
XLA Modules:
  0.0 66.3 jit_solution(9357740438676062297)
XLA Ops:
  0.7 64.0 %fused.1 = f32[64,1024]{1,0:T(8,128)} custom-call(bf16[8,128,128]{2,1,0:T(8,128)(2,1)} %own.1, f32[2,256]{1,0:T(2,128)} %coords.1, s32[1,8]{1,0:T(1,128)} %bitcast.5, s32[1,8]{1,0:T(1,128)} %bitcast.6, s32[1,1]{1,0:T(1,128)} %bitcast.4.count_in, f32[1,64]{1,0:T(1,128)} %bitcast.7), custom_call_target="tpu_custom_call" | custom-call | tf_op jit(solution)/shard_map/fused/pallas_call | solution.py:645
  64.7 1.7 %copy.9 = f32[64,1024]{1,0:T(8,128)} copy(f32[64,1024]{1,0:T(8,128)} %fused.1) | data formatting | bytes 524288

commit v5 on v4

--- a/solution.py
+++ b/solution.py
@@ -529,7 +529,7 @@
             copy.wait()
 
     def on_block(q, ch):
-        @pl.loop(0, part)
+        @pl.loop(0, part, unroll=part)
         def _(s):
             t = q * slots + ch * part + s
             products[t] = lax.dot_general(
@@ -552,21 +552,25 @@
     @pl.loop(0, homes // step_rows)
     def _(i):
         strip = pl.ds(pl.multiple_of(i * step_rows, step_rows), step_rows)
-        inner = pl.ds(pl.multiple_of((i % steps) * step_rows, step_rows), step_rows)
         running = jnp.zeros((step_rows, TILE), jnp.float32)
         for n in range(total):
             running = running * share_s[0, n] + products[whole_s[0, n], strip, :]
             runs[n] = running
         for r in range(row_tiles):
-            spread = [runs[whole_s[1, r * WEEKS + w]] for w in range(WEEKS)]
-            ahead = [spread[0]]
-            for w in range(1, WEEKS):
-                ahead.append(spread[w] + decay * ahead[-1])
-            back = None
-            for w in reversed(range(WEEKS)):
-                value = ahead[w] if back is None else ahead[w] + back
-                weighted[w, i // steps, inner, r * TILE : (r + 1) * TILE] = value.astype(jnp.bfloat16)
-                back = decay * (spread[w] if back is None else spread[w] + back)
+            ends = [whole_s[1, r * WEEKS + w] for w in range(WEEKS)]
+            for k in range(step_rows // 16):
+                spread = [runs[end, k * 16 : (k + 1) * 16, :] for end in ends]
+                ahead = [spread[0]]
+                for w in range(1, WEEKS):
+                    ahead.append(spread[w] + decay * ahead[-1])
+                back = None
+                lines_at = pl.ds(pl.multiple_of((i % steps) * step_rows + k * 16, 16), 16)
+                for w in reversed(range(WEEKS)):
+                    value = ahead[w] if back is None else ahead[w] + back
+                    weighted[w, i // steps, lines_at, r * TILE : (r + 1) * TILE] = value.astype(
+                        jnp.bfloat16
+                    )
+                    back = decay * (spread[w] if back is None else spread[w] + back)
 
     width = OBS // SPLIT
 
@@ -576,7 +580,7 @@
     def prepare(h):
         home_runs[h, 2 * slots] = jnp.zeros((TILE, width), jnp.float32)
 
-        @pl.loop(0, 2 * slots, unroll=4)
+        @pl.loop(0, 2 * slots, unroll=2 * slots)
         def _(n):
             value = jnp.dot(
                 home_tiles[whole_s[3, n]],

time: 66.5 us -> 63.1 us (0.949)
  Pallas kernels: 64 us -> 60.6 us
    pallas_call x1, Pallas kernels: 64 us -> 60.6 us  [local(): pl.pallas_call(functools.partial(fused_kernel, chips, lines), out_shape=j...]
where the time goes in v5:
time: 63.1 us; the launch traced here: 62.9 us
  Pallas kernels  60.6 us (96%)
  local copies, waits for them, and re-layouts  1.67 us (3%)
  between operations  0.66 us (1%)
    pallas_call x1, Pallas kernels, local(): pl.pallas_call(functools.partial(fused_kernel, chips, lines), out_shape=j...  60.6 us
    unnamed x1, local copies, waits for them, and re-layouts  1.67 us

profile of v5, /device:TPU:0, one launch (start us, length us, event | category | flops | bytes accessed | tf_op | source)
XLA Modules:
  0.0 62.9 jit_solution(17955370109334756722)
XLA Ops:
  0.7 60.6 %fused.1 = f32[64,1024]{1,0:T(8,128)} custom-call(bf16[8,128,128]{2,1,0:T(8,128)(2,1)} %own.1, f32[2,256]{1,0:T(2,128)} %coords.1, s32[1,8]{1,0:T(1,128)} %bitcast.5, s32[1,8]{1,0:T(1,128)} %bitcast.6, s32[1,1]{1,0:T(1,128)} %bitcast.4.count_in, f32[1,64]{1,0:T(1,128)} %bitcast.7), custom_call_target="tpu_custom_call" | custom-call | tf_op jit(solution)/shard_map/fused/pallas_call | solution.py:649
  61.3 1.7 %copy.9 = f32[64,1024]{1,0:T(8,128)} copy(f32[64,1024]{1,0:T(8,128)} %fused.1) | data formatting | bytes 524288
